TPU v7x, 256 devices: a whole 4x4x8 slice. The times are simulated.
256 devices in a mesh: grp: 4 (over x), seq: 16 (over z, core), mp: 4 (over y).
Axes of the slice: x: 4, y: 4, z: 8, core: 2. Of those that a mesh axis runs over, the one named last changes fastest.
Arguments:
- dec_query: bfloat16 [4, 4096, 4096], P('grp', 'seq', 'mp'), may hold values from -6 to 6
- dec_key: bfloat16 [4, 4096, 4096], P('grp', 'seq', 'mp'), may hold values from -6 to 6
- dec_value: bfloat16 [4, 4096, 4096], P('grp', 'seq', 'mp'), may hold values from -6 to 6
- cross_query: bfloat16 [4, 4096, 4096], P('grp', 'seq', 'mp'), may hold values from -6 to 6
- enc_query: bfloat16 [512, 128, 4096], P(('grp', 'seq', 'mp')), may hold values from -6 to 6
- enc_key: bfloat16 [512, 128, 4096], P(('grp', 'seq', 'mp')), may hold values from -6 to 6
- enc_value: bfloat16 [512, 128, 4096], P(('grp', 'seq', 'mp')), may hold values from -6 to 6
- nbr_index: int32 [4, 64, 2], P('grp', 'seq'), may hold values from 0 to 511, as said below
- seq_lengths: int32 [4], P('grp'), may hold values from 1024 to 4096, as said below
Outputs:
- self_attended: bfloat16 [4, 4096, 4096], P('grp', 'seq', 'mp')
- cross_attended: bfloat16 [4, 4096, 4096], P('grp', 'seq', 'mp')
Inputs may be any that keep to these rules, and one draw needn't show every extreme that they name: `nbr_index`: for the spans of candidate c on seq block s (spans s * 4 to s * 4 + 3), every id n has (n // 8) % 16 == s; among these 8 ids at most 4 share the value n // 128, and one value is shared by exactly 4; the two ids of a span differ. `seq_lengths`: some candidate has exactly 4096 valid tokens.
All inputs are finite; a program needn't handle non-finite values.
Results may differ from a plain program's by a relative error of at most 0.017.
Values may be sent and summed in bfloat16 or wider, within the bound.
A program may use at most 192 MiB of HBM per device.

v0:
```python
import jax
import jax.numpy as jnp
from jax import lax
from jax.sharding import PartitionSpec as P

HS = 128
SPAN = 64
NEIGH_K = 2
CAP = 4


MASKED = -1e30


def from_behind(x, axis, by):
    size = lax.axis_size(axis)
    pairs = [(i, i + by) for i in range(size) if 0 <= i + by < size]
    return lax.ppermute(x, axis, pairs)


def softmax_mix(query_heads, key_heads, value_heads):
    score_scale = HS ** (-0.5)
    scores = (
        jnp.einsum("gqhd,gkhd->ghqk", query_heads, key_heads, preferred_element_type=jnp.float32)
        * score_scale
    )
    row_top = jnp.max(scores, axis=3, keepdims=True)
    weights = jnp.exp(scores - row_top).astype(jnp.bfloat16)
    row_total = jnp.sum(weights, axis=3, dtype=jnp.float32)
    blended = jnp.einsum(
        "ghqk,gkhd->gqhd", weights, value_heads, preferred_element_type=jnp.float32
    )
    return blended / jnp.transpose(row_total, (0, 2, 1))[..., None]


def encode_block(queries, keys_in, values_in):
    stored, tokens, feature_width = queries.shape
    head_count = feature_width // HS
    shape_heads = (stored, tokens, head_count, HS)
    blended = softmax_mix(
        queries.reshape(shape_heads), keys_in.reshape(shape_heads), values_in.reshape(shape_heads)
    )
    blended = blended.reshape(stored, tokens, feature_width)
    new_keys = (keys_in.astype(jnp.float32) + blended).astype(jnp.bfloat16)
    new_values = (values_in.astype(jnp.float32) + blended).astype(jnp.bfloat16)
    return (new_keys, new_values)


def cross_mix(grouped, key_sets, value_sets):
    group_count, group_rows, feature_width = grouped.shape
    head_count = feature_width // HS
    set_rows = key_sets.shape[1]
    blended = softmax_mix(
        grouped.reshape(group_count, group_rows, head_count, HS),
        key_sets.reshape(group_count, set_rows, head_count, HS),
        value_sets.reshape(group_count, set_rows, head_count, HS),
    )
    return blended.reshape(group_count * group_rows, feature_width)


def local(
    dec_query,
    dec_key,
    dec_value,
    cross_query,
    enc_query,
    enc_key,
    enc_value,
    nbr_index,
    seq_lengths,
):
    row_count = dec_query.shape[1]
    feature_width = dec_query.shape[2]
    head_count = feature_width // HS
    first_row = lax.axis_index("seq") * row_count
    seq_length = seq_lengths[0]
    query_pos = first_row + jnp.arange(row_count, dtype=jnp.int32)
    pool_query, pool_key, pool_value = (
        lax.all_to_all(enc_query, "mp", split_axis=2, concat_axis=0, tiled=True),
        lax.all_to_all(enc_key, "mp", split_axis=2, concat_axis=0, tiled=True),
        lax.all_to_all(enc_value, "mp", split_axis=2, concat_axis=0, tiled=True),
    )
    pool_keys, pool_values = encode_block(pool_query, pool_key, pool_value)
    span_count = nbr_index.shape[1]
    request_count = span_count * NEIGH_K
    wanted = nbr_index.reshape(request_count)
    pool_size = pool_keys.shape[0]
    group_count = lax.axis_size("grp")
    column_size = lax.axis_size("seq") * pool_size
    target = wanted // column_size
    local_ids = wanted % pool_size
    order_ids = jnp.arange(request_count, dtype=jnp.int32)
    earlier = (target[None, :] == target[:, None]) & (order_ids[None, :] < order_ids[:, None])
    slot_rank = jnp.sum(earlier.astype(jnp.int32), axis=1)
    slot_ids = target * CAP + slot_rank
    tail_shape = pool_keys.shape[1:]
    slot_hits = slot_ids[:, None] == jnp.arange(group_count * CAP, dtype=jnp.int32)[None, :]
    asked_ids = jnp.sum(jnp.where(slot_hits, local_ids[:, None], 0), axis=0).reshape(
        group_count, CAP
    )
    arrived = lax.all_to_all(asked_ids, "grp", split_axis=0, concat_axis=0, tiled=True)
    picked = arrived.reshape(group_count * CAP)
    send_keys = pool_keys[picked].reshape((group_count, CAP) + tail_shape)
    send_values = pool_values[picked].reshape((group_count, CAP) + tail_shape)
    back_keys, back_values = (
        lax.all_to_all(send_keys, "grp", split_axis=0, concat_axis=0, tiled=True),
        lax.all_to_all(send_values, "grp", split_axis=0, concat_axis=0, tiled=True),
    )
    nbr_keys = back_keys.reshape((group_count * CAP,) + tail_shape)[slot_ids]
    nbr_values = back_values.reshape((group_count * CAP,) + tail_shape)[slot_ids]
    set_shape = (span_count, NEIGH_K * tail_shape[0], feature_width)
    key_sets = nbr_keys.reshape(set_shape)
    value_sets = nbr_values.reshape(set_shape)
    own_query = cross_query[0]
    prior = from_behind(jnp.stack([key_sets[-1:], value_sets[-1:]]), "seq", 1)
    all_keys = jnp.concatenate([prior[0], key_sets], axis=0)
    all_values = jnp.concatenate([prior[1], value_sets], axis=0)
    padded = jnp.concatenate(
        [
            jnp.zeros((1, feature_width), jnp.bfloat16),
            own_query,
            jnp.zeros((SPAN - 1, feature_width), jnp.bfloat16),
        ],
        axis=0,
    )
    blended = cross_mix(
        padded.reshape(span_count + 1, SPAN, feature_width), all_keys, all_values
    ).astype(jnp.bfloat16)
    cross_out = blended[1 : row_count + 1]
    live_cross = (query_pos >= SPAN - 1) & (query_pos < seq_length)
    cross_out = jnp.where(live_cross[:, None], cross_out, jnp.zeros_like(cross_out))
    query_heads = dec_query[0].reshape(row_count, head_count, HS)
    last_row = first_row + row_count - 1
    score_scale = HS ** (-0.5)
    initial = (
        jnp.full((head_count, row_count), MASKED, jnp.float32),
        jnp.zeros((head_count, row_count), jnp.float32),
        jnp.zeros((head_count, row_count, HS), jnp.float32),
    )
    key_start = jnp.int32(0)
    key_block = lax.all_gather(dec_key, "seq", axis=1, tiled=True)
    value_block = lax.all_gather(dec_value, "seq", axis=1, tiled=True)
    key_count = key_block.shape[1]

    def absorb(state_in):
        row_top, row_total, row_sum = state_in
        key_heads = key_block[0].reshape(key_count, head_count, HS)
        value_heads = value_block[0].reshape(key_count, head_count, HS)
        scores = (
            jnp.einsum("qhd,khd->hqk", query_heads, key_heads, preferred_element_type=jnp.float32)
            * score_scale
        )
        key_pos = jnp.arange(key_count, dtype=jnp.int32)
        allowed = (key_pos[None, :] <= query_pos[:, None]) & (key_pos[None, :] < seq_length)
        scores = jnp.where(allowed[None], scores, MASKED)
        new_top = jnp.maximum(row_top, jnp.max(scores, axis=2))
        weights = jnp.where(allowed[None], jnp.exp(scores - new_top[:, :, None]), 0.0).astype(
            jnp.bfloat16
        )
        row_total = jnp.sum(weights, axis=2, dtype=jnp.float32)
        row_sum = jnp.einsum(
            "hqk,khd->hqd", weights, value_heads, preferred_element_type=jnp.float32
        )
        return (new_top, row_total, row_sum)

    skipped = (key_start > last_row) | (key_start >= seq_length)
    final_top, final_total, final_sum = lax.cond(
        skipped, lambda state_in: state_in, absorb, initial
    )
    self_out = jnp.transpose(final_sum / final_total[:, :, None], (1, 0, 2)).reshape(
        row_count, feature_width
    )
    live_self = query_pos < seq_length
    self_out = jnp.where(live_self[:, None], self_out, 0.0).astype(jnp.bfloat16)
    return (self_out[None], cross_out[None])


def solution(mesh):
    return jax.shard_map(
        local,
        mesh=mesh,
        in_specs=(
            P("grp", "seq", "mp"),
            P("grp", "seq", "mp"),
            P("grp", "seq", "mp"),
            P("grp", "seq", "mp"),
            P(("grp", "seq", "mp"), None, None),
            P(("grp", "seq", "mp"), None, None),
            P(("grp", "seq", "mp"), None, None),
            P("grp", "seq", None),
            P("grp"),
        ),
        out_specs=(P("grp", "seq", "mp"), P("grp", "seq", "mp")),
        check_vma=False,
    )
```

profile of v0, /device:TPU:1, one launch (start us, length us, event | category | flops | bytes accessed | tf_op | source)
XLA Modules:
  0.0 349.0 jit_solution(1724088288305252603)
XLA Ops:
  7.2 0.7 all-gather.3.cloned.1.call-update
  7.9 0.7 all-gather.5.cloned.1.call-update
  8.6 0.8 copy.134
  9.8 0.7 all_to_all.54
  10.5 4.8 %all-to-all-start.3 = ((s32[4,1,4]{2,1,0:T(1,128)}), s32[4,1,4]{2,1,0:T(1,128)S(1)}, u32[]{:S(2)}, u32[]{:S(2)}) async-start(s32[4,1,4]{2,1,0:T(1,128)} %bitcast.16), calls=%async_computation.3 | async-start | bytes 4096 | tf_op jit(solution)/shard_map/all_to_all | solution.py:101
  15.3 6.1 %copy.130 = bf16[2,128,4096]{1,0,2:T(2,128)(2,1)} copy(bf16[2,128,4096]{2,1,0:T(8,128)(2,1)} %param.17) | data formatting | bytes 4194304 | tf_op args[6]
  21.4 4.2 %all-to-all-start.2 = ((bf16[2,128,4096]{1,0,2:T(2,128)(2,1)}), bf16[2,128,4096]{1,0,2:T(2,128)(2,1)S(1)}, u32[]{:S(2)}, u32[]{:S(2)}) async-start(bf16[2,128,4096]{1,0,2:T(2,128)(2,1)} %copy.130), calls=%async_computation.2 | async-start | bytes 4194304 | tf_op jit(solution)/shard_map/all_to_all | solution.py:81
  25.6 6.2 %copy.124 = bf16[2,128,4096]{1,0,2:T(2,128)(2,1)} copy(bf16[2,128,4096]{2,1,0:T(8,128)(2,1)} %param.15) | data formatting | bytes 4194304 | tf_op args[4]
  31.8 19.0 %all-to-all-done.2 = bf16[2,128,4096]{1,0,2:T(2,128)(2,1)S(1)} async-done(((bf16[2,128,4096]{1,0,2:T(2,128)(2,1)}), bf16[2,128,4096]{1,0,2:T(2,128)(2,1)S(1)}, u32[]{:S(2)}, u32[]{:S(2)}) %all-to-all-start.2) | async-done | bytes 2097184 | tf_op jit(solution)/shard_map/all_to_all | solution.py:81
  50.7 4.5 %all-to-all-start.1 = ((bf16[2,128,4096]{1,0,2:T(2,128)(2,1)}), bf16[2,128,4096]{1,0,2:T(2,128)(2,1)}, u32[]{:S(2)}, u32[]{:S(2)}) async-start(bf16[2,128,4096]{1,0,2:T(2,128)(2,1)} %copy.124), calls=%async_computation.1 | async-start | bytes 4194304 | tf_op jit(solution)/shard_map/all_to_all | solution.py:79
  55.2 6.2 %copy.121 = bf16[2,128,4096]{1,0,2:T(2,128)(2,1)} copy(bf16[2,128,4096]{2,1,0:T(8,128)(2,1)} %param.16) | data formatting | bytes 4194304 | tf_op args[5]
  61.4 18.1 %all-to-all-done.1 = bf16[2,128,4096]{1,0,2:T(2,128)(2,1)} async-done(((bf16[2,128,4096]{1,0,2:T(2,128)(2,1)}), bf16[2,128,4096]{1,0,2:T(2,128)(2,1)}, u32[]{:S(2)}, u32[]{:S(2)}) %all-to-all-start.1) | async-done | bytes 2097184 | tf_op jit(solution)/shard_map/all_to_all | solution.py:79
  79.5 4.5 %all-to-all-start = ((bf16[2,128,4096]{1,0,2:T(2,128)(2,1)}), bf16[2,128,4096]{1,0,2:T(2,128)(2,1)}, u32[]{:S(2)}, u32[]{:S(2)}) async-start(bf16[2,128,4096]{1,0,2:T(2,128)(2,1)} %copy.121), calls=%async_computation | async-start | bytes 4194304 | tf_op jit(solution)/shard_map/all_to_all | solution.py:80
  83.9 0.5 broadcast.320
  84.5 0.7 reduce.3
  85.2 1.6 copy.131
  86.8 1.9 copy.125
  88.7 1.5 copy.126
  90.2 17.0 %all-to-all-done = bf16[2,128,4096]{1,0,2:T(2,128)(2,1)} async-done(((bf16[2,128,4096]{1,0,2:T(2,128)(2,1)}), bf16[2,128,4096]{1,0,2:T(2,128)(2,1)}, u32[]{:S(2)}, u32[]{:S(2)}) %all-to-all-start) | async-done | bytes 2097184 | tf_op jit(solution)/shard_map/all_to_all | solution.py:80
  107.3 2.1 copy.122
  109.6 0.9 multiply_reduce_fusion
  110.5 1.0 convert_reduce_fusion.1
  111.5 0.7 copy-done.2
  112.2 0.9 bitcast_divide_fusion
  113.1 2.0 copy-done
  115.1 2.0 fusion.7
  117.1 4.7 %gather_fusion.2 = bf16[16,128,1024]{1,2,0:T(8,128)(2,1)} fusion(bf16[8,128,1024]{1,2,0:T(8,128)(2,1)} %fusion.7, s32[1024]{0:T(1024)S(1)} %pad_clamp_fusion.1), kind=kCustom, calls=%fused_computation.2 | custom fusion | bytes 8388672 | tf_op jit(solution)/shard_map/gather | solution.py:104
  121.8 6.4 %copy.137 = bf16[4,4,128,1024]{3,2,1,0:T(8,128)(2,1)} copy(bf16[4,4,128,1024]{2,3,1,0:T(8,128)(2,1)} %bitcast.89) | data formatting | bytes 8388608 | tf_op jit(solution)/shard_map/reshape | solution.py:104
  128.1 4.8 %all-to-all-start.5 = ((bf16[4,4,128,1024]{3,2,1,0:T(8,128)(2,1)}), bf16[4,4,128,1024]{3,2,1,0:T(8,128)(2,1)}, u32[]{:S(2)}, u32[]{:S(2)}) async-start(bf16[4,4,128,1024]{3,2,1,0:T(8,128)(2,1)} %copy.137), calls=%async_computation.5 | async-start | bytes 8388608 | tf_op jit(solution)/shard_map/all_to_all | solution.py:107
  133.0 3.1 copy.123
  136.1 5.3 %copy.133 = f32[8,128,1024]{2,1,0:T(8,128)} copy(f32[8,128,1024]{1,2,0:T(8,128)} %bitcast.88) | data formatting | bytes 8388608 | tf_op jit(solution)/shard_map/reshape | solution.py:43
  141.5 4.2 %fusion.8 = bf16[8,128,1024]{2,1,0:T(8,128)(2,1)S(1)} fusion(f32[8,128,1024]{2,1,0:T(8,128)} %copy.133, f32[4,2,128,1024]{3,2,1,0:T(8,128)} %copy.123), kind=kLoop, calls=%fused_computation.22 | loop fusion | flops 2097152 | bytes 10485760 | tf_op jit(solution)/shard_map/convert_element_type | solution.py:44
  145.7 2.8 gather_fusion
  148.4 29.6 %all-to-all-done.5 = bf16[4,4,128,1024]{3,2,1,0:T(8,128)(2,1)} async-done(((bf16[4,4,128,1024]{3,2,1,0:T(8,128)(2,1)}), bf16[4,4,128,1024]{3,2,1,0:T(8,128)(2,1)}, u32[]{:S(2)}, u32[]{:S(2)}) %all-to-all-start.5) | async-done | bytes 4194336 | tf_op jit(solution)/shard_map/all_to_all | solution.py:107
  178.0 4.8 %all-to-all-start.4 = ((bf16[4,4,128,1024]{3,2,1,0:T(8,128)(2,1)}), bf16[4,4,128,1024]{3,2,1,0:T(8,128)(2,1)}, u32[]{:S(2)}, u32[]{:S(2)}) async-start(bf16[4,4,128,1024]{3,2,1,0:T(8,128)(2,1)} %bitcast.87), calls=%async_computation.4 | async-start | bytes 8388608 | tf_op jit(solution)/shard_map/all_to_all | solution.py:106
  182.9 2.9 gather_fusion.3
  185.9 41.0 %all-to-all-done.4 = bf16[4,4,128,1024]{3,2,1,0:T(8,128)(2,1)} async-done(((bf16[4,4,128,1024]{3,2,1,0:T(8,128)(2,1)}), bf16[4,4,128,1024]{3,2,1,0:T(8,128)(2,1)}, u32[]{:S(2)}, u32[]{:S(2)}) %all-to-all-start.4) | async-done | bytes 4194336 | tf_op jit(solution)/shard_map/all_to_all | solution.py:106
  226.9 4.2 %gather_fusion.1 = bf16[8,128,1024]{2,1,0:T(8,128)(2,1)} fusion(bf16[16,128,1024]{2,1,0:T(8,128)(2,1)} %bitcast.19, s32[1024]{0:T(1024)S(1)} %pad_clamp_fusion), kind=kCustom, calls=%fused_computation.1 | custom fusion | bytes 4194336 | tf_op jit(solution)/shard_map/gather | solution.py:109
  231.1 1.1 slice.30
  232.2 1.1 pad_maximum_fusion
  233.3 9.1 %collective-permute-start = (bf16[2,1,256,1024]{3,2,1,0:T(8,128)(2,1)}, bf16[2,1,256,1024]{3,2,1,0:T(8,128)(2,1)}, u32[]{:S(2)}, u32[]{:S(2)}) collective-permute-start(bf16[2,1,256,1024]{3,2,1,0:T(8,128)(2,1)} %pad_maximum_fusion), channel_id=1, source_target_pairs={{0,4},{4,8},{8,12},{12,16},{16,20},{20,24},{24,28},{28,32},{32,36}... | collective-permute-start | bytes 3145736 | tf_op jit(solution)/shard_map/ppermute | solution.py:18
  243.4 1.0 copy.152
  244.4 0.6 copy.154
  245.0 0.5 copy.140
  245.5 0.5 copy-done.1
  246.0 0.6 copy.153
  246.6 1.8 copy.143
  248.4 5.8 %collective-permute-done = bf16[2,1,256,1024]{3,2,1,0:T(8,128)(2,1)} collective-permute-done((bf16[2,1,256,1024]{3,2,1,0:T(8,128)(2,1)}, bf16[2,1,256,1024]{3,2,1,0:T(8,128)(2,1)}, u32[]{:S(2)}, u32[]{:S(2)}) %collective-permute-start) | collective-permute-done | bytes 1048608 | tf_op jit(solution)/shard_map/ppermute | solution.py:18
  254.2 2.1 fusion.32
  256.3 1.2 copy.138
  257.5 1.0 copy.139
  259.0 3.0 multiply_reduce_fusion.1
  262.0 0.9 convert_reduce_fusion.2
  262.9 1.1 divide_convert_fusion
  264.6 1.0 fusion.23
  265.5 74.7 %conditional.1 = (f32[8,256]{1,0:T(8,128)S(1)}, f32[8,256,128]{2,1,0:T(8,128)S(1)}) conditional(s32[]{:T(128)} %convert_element_type.58, (s32[]{:T(128)}, s32[256]{0:T(256)S(1)}, s32[]{:T(128)}, bf16[1,256,1024]{2,1,0:T(8,128)(2,1)S(1)}, bf16[1,4096,1024]{2,1,0:T(8,128)(2,1)}, /*index=5*/bf16[1,4096,1024]{2,1,0:T(8,128)(2,1)}) %tuple.31, () %tuple.17), branch_computations={%region_0.3_spmd, %region_3.4_spmd} | conditional | flops 4422895616 | bytes 157871120 | solution.py:167
  265.8 0.7 iota_compare_fusion.1
  266.4 0.8 fusion.5
  267.2 8.8 %copy.150 = bf16[512,8,8,128]{3,2,1,0:T(8,128)(2,1)} copy(bf16[512,8,8,128]{3,1,2,0:T(8,128)(2,1)} %bitcast.92) | data formatting | bytes 16777216 | tf_op jit(solution)/shard_map/cond
  276.1 19.0 %fusion = (f32[8,256]{1,0:T(8,128)S(1)}, f32[8,256,4096]{2,1,0:T(8,128)}) fusion(pred[256,4096]{1,0:T(8,128)(4,1)S(1)} %fusion.5, bf16[4096,8,128]{2,1,0:T(8,128)(2,1)} %bitcast.94, bf16[256,8,128]{2,1,0:T(8,128)(2,1)S(1)} %bitcast.112), kind=kOutput, calls=%fused_computation.7 | convolution fusion | flops 2172647424 | bytes 43524096 | tf_op jit(solution)/shard_map/cond/branch_0_fun/qhd,khd->hqk/dot_general | solution.py:150
  295.1 16.1 %convert_reduce_fusion = f32[8,256]{1,0:T(8,128)S(1)} fusion(f32[8,256]{1,0:T(8,128)S(1)} %broadcast_maximum_fusion, f32[8,256,4096]{2,1,0:T(8,128)} %get-tuple-element.30, pred[256,4096]{1,0:T(8,128)(4,1)S(1)} %fusion.5), kind=kLoop, calls=%fused_computation.4 | loop fusion | flops 58718208 | bytes 34619392 | tf_op jit(solution)/shard_map/cond/branch_0_fun/reduce_sum | solution.py:160
  311.2 8.8 %copy.151 = bf16[512,8,8,128]{3,2,1,0:T(8,128)(2,1)} copy(bf16[512,8,8,128]{3,1,2,0:T(8,128)(2,1)} %bitcast.93) | data formatting | bytes 16777216 | tf_op jit(solution)/shard_map/cond
  320.0 20.0 %fusion.1 = f32[8,256,128]{2,1,0:T(8,128)S(1)} fusion(bf16[4096,8,128]{2,1,0:T(8,128)(2,1)} %bitcast.95, f32[8,256,4096]{2,1,0:T(8,128)} %get-tuple-element.30, f32[8,256]{1,0:T(8,128)S(1)} %broadcast_maximum_fusion, pred[256,4096]{1,0:T(8,128)(4,1)S(1)} %fusion.5), kind=kOutput, calls=%fused_computation.8 | convolution fusion | flops 2189426688 | bytes 44048384 | tf_op jit(solution)/shard_map/cond/branch_0_fun/hqk,khd->hqd/dot_general | solution.py:161
  341.2 1.0 select_convert_fusion.2
  (45 shorter events, 3.3 us)
Async XLA Ops:
  7.2 258.4 %all-gather.3.cloned.1.call-start = ((), (), s32[]{:S(2)}) async-start(), calls=%async_computation.6 | async-start | bytes 8912896 | tf_op jit(solution)/shard_map/all_gather | solution.py:141
  7.9 257.6 %all-gather.5.cloned.1.call-start = ((), (), s32[]{:S(2)}) async-start(), calls=%async_computation.7 | async-start | bytes 8912896 | tf_op jit(solution)/shard_map/all_gather | solution.py:142
  10.5 11.0 %all-to-all-start.3 = ((s32[4,1,4]{2,1,0:T(1,128)}), s32[4,1,4]{2,1,0:T(1,128)S(1)}, u32[]{:S(2)}, u32[]{:S(2)}) async-start(s32[4,1,4]{2,1,0:T(1,128)} %bitcast.16), calls=%async_computation.3 | async-start | bytes 4096 | tf_op jit(solution)/shard_map/all_to_all | solution.py:101
  21.4 29.3 %all-to-all-start.2 = ((bf16[2,128,4096]{1,0,2:T(2,128)(2,1)}), bf16[2,128,4096]{1,0,2:T(2,128)(2,1)S(1)}, u32[]{:S(2)}, u32[]{:S(2)}) async-start(bf16[2,128,4096]{1,0,2:T(2,128)(2,1)} %copy.130), calls=%async_computation.2 | async-start | bytes 4194304 | tf_op jit(solution)/shard_map/all_to_all | solution.py:81
  50.7 28.7 %all-to-all-start.1 = ((bf16[2,128,4096]{1,0,2:T(2,128)(2,1)}), bf16[2,128,4096]{1,0,2:T(2,128)(2,1)}, u32[]{:S(2)}, u32[]{:S(2)}) async-start(bf16[2,128,4096]{1,0,2:T(2,128)(2,1)} %copy.124), calls=%async_computation.1 | async-start | bytes 4194304 | tf_op jit(solution)/shard_map/all_to_all | solution.py:79
  79.5 27.8 %all-to-all-start = ((bf16[2,128,4096]{1,0,2:T(2,128)(2,1)}), bf16[2,128,4096]{1,0,2:T(2,128)(2,1)}, u32[]{:S(2)}, u32[]{:S(2)}) async-start(bf16[2,128,4096]{1,0,2:T(2,128)(2,1)} %copy.121), calls=%async_computation | async-start | bytes 4194304 | tf_op jit(solution)/shard_map/all_to_all | solution.py:80
  107.3 2.3 copy-start.3
  110.5 1.7 copy-start.2
  113.1 2.0 copy-start
  128.1 49.8 %all-to-all-start.5 = ((bf16[4,4,128,1024]{3,2,1,0:T(8,128)(2,1)}), bf16[4,4,128,1024]{3,2,1,0:T(8,128)(2,1)}, u32[]{:S(2)}, u32[]{:S(2)}) async-start(bf16[4,4,128,1024]{3,2,1,0:T(8,128)(2,1)} %copy.137), calls=%async_computation.5 | async-start | bytes 8388608 | tf_op jit(solution)/shard_map/all_to_all | solution.py:107
  178.0 48.9 %all-to-all-start.4 = ((bf16[4,4,128,1024]{3,2,1,0:T(8,128)(2,1)}), bf16[4,4,128,1024]{3,2,1,0:T(8,128)(2,1)}, u32[]{:S(2)}, u32[]{:S(2)}) async-start(bf16[4,4,128,1024]{3,2,1,0:T(8,128)(2,1)} %bitcast.87), calls=%async_computation.4 | async-start | bytes 8388608 | tf_op jit(solution)/shard_map/all_to_all | solution.py:106
  185.8 57.3 %copy-start.4 = (bf16[1,256,1024]{2,1,0:T(8,128)(2,1)S(1)}, bf16[1,256,1024]{2,1,0:T(8,128)(2,1)}, u32[]{:S(2)}) copy-start(bf16[1,256,1024]{2,1,0:T(8,128)(2,1)} %param.14) | copy-start | bytes 1572868
  233.3 20.9 %collective-permute-start = (bf16[2,1,256,1024]{3,2,1,0:T(8,128)(2,1)}, bf16[2,1,256,1024]{3,2,1,0:T(8,128)(2,1)}, u32[]{:S(2)}, u32[]{:S(2)}) collective-permute-start(bf16[2,1,256,1024]{3,2,1,0:T(8,128)(2,1)} %pad_maximum_fusion), channel_id=1, source_target_pairs={{0,4},{4,8},{8,12},{12,16},{16,20},{20,24},{24,28},{28,32},{32,36}... | collective-permute-start | bytes 3145736 | tf_op jit(solution)/shard_map/ppermute | solution.py:18
  244.4 1.6 copy-start.1
  259.0 3.9 %copy-start.6 = (bf16[1,256,8,128]{3,1,2,0:T(8,128)(2,1)S(1)}, bf16[1,256,8,128]{3,1,2,0:T(8,128)(2,1)}, u32[]{:S(2)}) copy-start(bf16[1,256,8,128]{3,1,2,0:T(8,128)(2,1)} %copy.139) | copy-start | bytes 1572868
  262.9 2.7 copy-start.5
Sparse Core Ops, SparseCore 0:
  9.8 60.1 all-gather.2
  71.8 54.4 all-gather.4
where the time goes:
time: 352 us; the launch traced here: 349 us
  waiting for transfers between devices  132 us (38%)
  local copies, waits for them, and re-layouts  89.7 us (25%)
  matrix products  44.9 us (13%)
  starting transfers between devices  36.8 us (10%)
  other arithmetic  30.2 us (9%)
  between operations  15 us (4%)
    all_to_all x1, waiting for transfers between devices, local(): lax.all_to_all(send_keys, 'grp', split_axis=0, concat_axis=0, tiled=True)  41 us
    all_to_all x1, waiting for transfers between devices, local(): lax.all_to_all(send_values, 'grp', split_axis=0, concat_axis=0, tiled=True)  29.6 us
    unnamed x22, local copies, waits for them, and re-layouts  24.7 us
    dot_general x1, matrix products, absorb(): jnp.einsum('hqk,khd->hqd', weights, value_heads, preferred_element_type=j...  20 us
    dot_general x1, matrix products, absorb(): jnp.einsum('qhd,khd->hqk', query_heads, key_heads, preferred_element_type...  19 us
    all_to_all x1, waiting for transfers between devices, local(): lax.all_to_all(enc_value, 'mp', split_axis=2, concat_axis=0, tiled=True)  19 us
    all_to_all x1, waiting for transfers between devices, local(): lax.all_to_all(enc_query, 'mp', split_axis=2, concat_axis=0, tiled=True)  18.1 us
    cond x3, local copies, waits for them, and re-layouts  17.6 us
  transfers between devices with their start and end apart: 9, of which 6 were waited for; matrix products, arithmetic and copies ran while one was open for 24% of the time, Pallas kernels for 0%

commit v1 on v0

v1 whole, which is shorter than its diff:
```python
import functools
import math

import jax
import jax.numpy as jnp
from jax import lax
from jax.experimental import pallas as pl
from jax.experimental.pallas import tpu as pltpu
from jax.sharding import PartitionSpec as P

HS = 128
SPAN = 64
CAP = 4
CHUNKS = 4
PAIR = 2 * HS
ROWS = 256
WIDTH = 1024
SCALE = HS ** (-0.5) * math.log2(math.e)
MASKED = -1e30
MESH = pl.DeviceIdType.MESH
F32 = jnp.float32
BF16 = jnp.bfloat16
NT = (((1,), (1,)), ((), ()))


def mod(a, n):
    return lax.rem(a, n)


def scores_of(q, k):
    return lax.dot_general(q, k, NT, preferred_element_type=F32)


def mix(weights, v):
    return jnp.dot(weights.astype(BF16), v, preferred_element_type=F32)


def kernel(
    nbr, lens, dq, dk, dv, cq, eq, ek, ev,
    self_out, cross_out,
    eqv, ekv, evv, cqv, halo, qf,
    kvs0, kvs1, kvs2, kvs3,
    pool0, pool1, pool2, pool3,
    qb0, qb1, qb2, qb3,
    os0, os1, os2, os3,
    ss0, ss1, ss2, ss3,
    stage, o_in, st_in, stat, of, tail_s, tail_in, co,
    qs, kf, vf, os_self,
    idx_s, idx_all, idx_sm, row_tab, id_tab, req_tab,
    load_sem, z_send, z_recv, f_send, f_recv, y_send, y_recv, y_loc,
    q_send, q_recv, o_send, o_recv, t_send, t_recv, i_send, i_recv,
    b_send, b_recv, h_send, h_recv, misc,
):
    kvs = (kvs0, kvs1, kvs2, kvs3)
    pool = (pool0, pool1, pool2, pool3)
    qb = (qb0, qb1, qb2, qb3)
    os = (os0, os1, os2, os3)
    ss = (ss0, ss1, ss2, ss3)
    g = lax.axis_index("grp")
    s = lax.axis_index("seq")
    m = lax.axis_index("mp")
    z = lax.div(s, 2)
    core = lax.rem(s, 2)
    seq_len = lens[0]

    def z_dev(zz):
        return (g, 2 * zz + core, m)

    def y_dev(mm):
        return (g, s, mm)

    def x_dev(gg):
        return (gg, s, m)

    partner = (g, s + 1 - 2 * core, m)
    other = (g, mod(s + 15 + 2 * core, 16), m)
    behind = (g, mod(s + 15, 16), m)
    ahead = (g, mod(s + 1, 16), m)

    def remote(src, dst, send, recv, dev):
        return pltpu.make_async_remote_copy(
            src_ref=src, dst_ref=dst, send_sem=send, recv_sem=recv,
            device_id=dev, device_id_type=MESH,
        )

    loads = [
        pltpu.make_async_copy(src, dst, load_sem.at[n])
        for n, (src, dst) in enumerate(((cq.at[0], cqv), (eq, eqv), (ek, ekv), (ev, evv)))
    ]
    for c in loads:
        c.start()
    own = pl.ds(pl.multiple_of(z * HS, HS), HS)
    local_in = [
        pltpu.make_async_copy(dq.at[0, :, own], qs.at[z], load_sem.at[4]),
        pltpu.make_async_copy(dk.at[0, :, own], kf.at[s], load_sem.at[5]),
        pltpu.make_async_copy(dv.at[0, :, own], vf.at[s], load_sem.at[6]),
    ]
    for c in local_in:
        c.start()

    bar = pltpu.get_barrier_semaphore()
    peers = [z_dev(mod(z + off, 8)) for off in range(1, 8)]
    peers += [y_dev(mod(m + off, 4)) for off in range(1, 4)]
    peers += [x_dev(mod(g + off, 4)) for off in range(1, 4)]
    peers += [partner, other]
    for dev in peers:
        pl.semaphore_signal(bar, inc=1, device_id=dev, device_id_type=MESH)
    pl.semaphore_wait(bar, len(peers))

    halo_copy = remote(cq.at[0, pl.ds(0, SPAN)], halo, h_send.at[0], h_recv.at[0], behind)
    halo_copy.start()

    lane8 = lax.broadcasted_iota(jnp.int32, (8, 128), 1)
    packed = jnp.zeros((8, 128), jnp.int32)
    for n in range(8):
        packed = jnp.where(lane8 == n, nbr[0, n // 2, n % 2], packed)
    idx_s[...] = packed
    idx_copies = [
        remote(idx_s, idx_all.at[g], i_send.at[off - 1], i_recv.at[off - 1], x_dev(mod(g + off, 4)))
        for off in range(1, 4)
    ]
    for c in idx_copies:
        c.start()
    idx_local = pltpu.make_async_copy(idx_s, idx_all.at[g], misc.at[0])
    idx_local.start()

    z_order = (4, 3, 5, 2, 6, 1, 7)

    def z_copies(off):
        zz = mod(z + off, 8)
        cols = pl.ds(pl.multiple_of(zz * HS, HS), HS)
        dev = z_dev(zz)
        n = (off - 1) * 3
        return (
            remote(dk.at[0, :, cols], kf.at[s], z_send.at[n], z_recv.at[n], dev),
            remote(dq.at[0, :, cols], qs.at[z], z_send.at[n + 1], z_recv.at[n + 1], dev),
            remote(dv.at[0, :, cols], vf.at[s], z_send.at[n + 2], z_recv.at[n + 2], dev),
        )

    def z_arrivals(off):
        zz = mod(z + 8 - off, 8)
        n = (off - 1) * 3
        dev = z_dev(zz)
        b = 2 * zz + core
        return (
            remote(kf.at[b], kf.at[b], z_send.at[n], z_recv.at[n], dev),
            remote(qs.at[zz], qs.at[zz], z_send.at[n + 1], z_recv.at[n + 1], dev),
            remote(vf.at[b], vf.at[b], z_send.at[n + 2], z_recv.at[n + 2], dev),
        )

    def forwards(off):
        b = 2 * mod(z + 8 - off, 8) + core
        n = off * 2
        return (
            remote(kf.at[b], kf.at[b], f_send.at[n], f_recv.at[n], partner),
            remote(vf.at[b], vf.at[b], f_send.at[n + 1], f_recv.at[n + 1], partner),
        )

    def forward_arrivals(off):
        b = 2 * mod(z + 8 - off, 8) + 1 - core
        n = off * 2
        return (
            remote(kf.at[b], kf.at[b], f_send.at[n], f_recv.at[n], partner),
            remote(vf.at[b], vf.at[b], f_send.at[n + 1], f_recv.at[n + 1], partner),
        )

    for part in range(3):
        for off in z_order:
            z_copies(off)[part].start()

    def y_copy(hc, off):
        return remote(
            kvs[hc].at[off], pool[hc].at[pl.ds(2 * m, 2)],
            y_send.at[hc * 3 + off], y_recv.at[hc * 3 + off], y_dev(mod(m + 1 + off, 4)),
        )

    def y_arrival(hc, off):
        mm = mod(m + 3 - off, 4)
        return remote(
            kvs[hc].at[off], pool[hc].at[pl.ds(2 * mm, 2)],
            y_send.at[hc * 3 + off], y_recv.at[hc * 3 + off], y_dev(mm),
        )

    def y_local(hc):
        return pltpu.make_async_copy(kvs[hc].at[3], pool[hc].at[pl.ds(2 * m, 2)], y_loc.at[hc])

    def encode(hc):
        out = kvs[hc]

        def step(off, carry):
            t = mod(m + 1 + off, 4)
            for n in range(2):
                for j in range(2):
                    cols = pl.ds(pl.multiple_of((t * 8 + hc * 2 + j) * HS, HS), HS)
                    q, k, v = eqv[n, :, cols], ekv[n, :, cols], evv[n, :, cols]
                    sc = scores_of(q, k)
                    top = jnp.max(sc, axis=1, keepdims=True)
                    w = jnp.exp2((sc - top) * SCALE)
                    inv = 1.0 / jnp.sum(w, axis=1, keepdims=True)
                    mixed = mix(w, v) * inv
                    at = slice(j * HS, (j + 1) * HS)
                    out[off, n, 0, :, at] = (k.astype(F32) + mixed).astype(BF16)
                    out[off, n, 1, :, at] = (v.astype(F32) + mixed).astype(BF16)

            @pl.when(off < 3)
            def _():
                y_copy(hc, off).start()

            @pl.when(off == 3)
            def _():
                y_local(hc).start()

            return carry

        lax.fori_loop(0, 4, step, 0)

    def q_copy(hc, off):
        mine = qb[hc].at[pl.ds(4 * g, 4)]
        return remote(
            mine, mine, q_send.at[hc * 3 + off], q_recv.at[hc * 3 + off], x_dev(mod(g + 1 + off, 4))
        )

    def q_arrival(hc, off):
        gg = mod(g + 3 - off, 4)
        theirs = qb[hc].at[pl.ds(4 * gg, 4)]
        return remote(
            theirs, theirs, q_send.at[hc * 3 + off], q_recv.at[hc * 3 + off], x_dev(gg)
        )

    def shift_queries():
        loads[0].wait()
        halo_copy.wait_recv()
        qf[0:ROWS, :] = cqv[...].astype(F32)
        qf[ROWS : ROWS + SPAN, :] = halo[...].astype(F32)
        for hc in range(CHUNKS):
            for u in range(4):
                first = SPAN - 1 + SPAN * u
                qb[hc][4 * g + u] = qf[first : first + SPAN, hc * PAIR : (hc + 1) * PAIR].astype(BF16)
            for off in range(3):
                q_copy(hc, off).start()

    def tables():
        for off in range(1, 4):
            gg = mod(g + 4 - off, 4)
            remote(
                idx_s, idx_all.at[gg], i_send.at[off - 1], i_recv.at[off - 1], x_dev(gg)
            ).wait_recv()
        idx_local.wait()
        to_smem = pltpu.make_async_copy(idx_all, idx_sm, misc.at[1])
        to_smem.start()
        to_smem.wait()

        def per_candidate(c, carry):
            ids = [idx_sm[c, 0, n] for n in range(8)]
            count = jnp.int32(0)
            rows = [c * 4] * CAP
            locals_ = [jnp.int32(0)] * CAP
            for n in range(8):
                mine = lax.shift_right_logical(ids[n], 7) == g
                for r in range(CAP):
                    hit = jnp.logical_and(mine, count == r)
                    rows[r] = jnp.where(hit, c * 4 + n // 2, rows[r])
                    locals_[r] = jnp.where(hit, ids[n] & 7, locals_[r])
                count = count + jnp.where(mine, 1, 0)
            for r in range(CAP):
                row_tab[c * 4 + r] = rows[r]
                id_tab[c * 4 + r] = locals_[r]
            return carry

        lax.fori_loop(0, 4, per_candidate, 0)
        targets = [lax.shift_right_logical(nbr[0, n // 2, n % 2], 7) for n in range(8)]
        for n in range(8):
            rank = jnp.int32(0)
            for e in range(n):
                rank = rank + jnp.where(targets[e] == targets[n], 1, 0)
            req_tab[n] = targets[n] * CAP + rank

    lane64 = lax.broadcasted_iota(jnp.int32, (SPAN, 128), 1)

    def o_copy(hc, off):
        return remote(
            os[hc].at[off], o_in.at[pl.ds(4 * g, 4), :, pl.ds(hc * PAIR, PAIR)],
            o_send.at[hc * 3 + off], o_recv.at[hc * 3 + off], x_dev(mod(g + 1 + off, 4)),
        )

    def t_copy(hc, off):
        return remote(
            ss[hc].at[off], st_in.at[4 * g + hc],
            t_send.at[hc * 3 + off], t_recv.at[hc * 3 + off], x_dev(mod(g + 1 + off, 4)),
        )

    def o_local(hc):
        return (
            pltpu.make_async_copy(
                os[hc].at[3], o_in.at[pl.ds(4 * g, 4), :, pl.ds(hc * PAIR, PAIR)], misc.at[2 + hc]
            ),
            pltpu.make_async_copy(ss[hc].at[3], st_in.at[4 * g + hc], misc.at[6 + hc]),
        )

    def cross(hc):
        for off in range(3):
            y_arrival(hc, off).wait_recv()
            q_arrival(hc, off).wait_recv()
        y_local(hc).wait()

        def step(off, carry):
            c = mod(g + 1 + off, 4)
            for r in range(CAP):
                row = row_tab[c * 4 + r]
                local = id_tab[c * 4 + r]
                q2 = qb[hc][row]
                k2 = pool[hc][local, 0]
                v2 = pool[hc][local, 1]
                logs = []
                for j in range(2):
                    at = slice(j * HS, (j + 1) * HS)
                    sc = scores_of(q2[:, at], k2[:, at])
                    top = jnp.max(sc, axis=1, keepdims=True)
                    w = jnp.exp2((sc - top) * SCALE)
                    total = jnp.sum(w, axis=1, keepdims=True)
                    os[hc][off, r, :, at] = (mix(w, v2[:, at]) * (1.0 / total)).astype(BF16)
                    logs.append(top * SCALE + jnp.log2(total))
                stage[r * SPAN : (r + 1) * SPAN, :] = jnp.where(
                    lane64 == 0, logs[0], jnp.where(lane64 == 1, logs[1], 0.0)
                )
            ss[hc][off] = jnp.transpose(stage[...])[0:8]

            @pl.when(off < 3)
            def _():
                o_copy(hc, off).start()
                t_copy(hc, off).start()

            @pl.when(off == 3)
            def _():
                for c_ in o_local(hc):
                    c_.start()

            return carry

        lax.fori_loop(0, 4, step, 0)

    def b_copy(i, k):
        return remote(
            os_self.at[i], self_out.at[0, :, own], b_send.at[k], b_recv.at[k], z_dev(i)
        )

    KEYS = 512
    key_iota = lax.broadcasted_iota(jnp.int32, (ROWS, KEYS), 1)
    row_iota = lax.broadcasted_iota(jnp.int32, (ROWS, KEYS), 0)

    def self_attend():
        def block(k, carry):
            i = mod(z + 1 + k, 8)
            q = qs[i]

            def keys_of(ref, j):
                return ref[pl.ds(2 * j, 2)].reshape(KEYS, HS)

            sc = scores_of(q, keys_of(kf, i))
            sc = jnp.where(key_iota <= row_iota + core * ROWS, sc, MASKED)
            top = jnp.max(sc, axis=1, keepdims=True)
            w = jnp.exp2((sc - top) * SCALE)
            total = jnp.sum(w, axis=1, keepdims=True)
            acc = mix(w, keys_of(vf, i))

            def step(j, state):
                top, total, acc = state
                sc = scores_of(q, keys_of(kf, j))
                new = jnp.maximum(top, jnp.max(sc, axis=1, keepdims=True))
                old = jnp.exp2((top - new) * SCALE)
                w = jnp.exp2((sc - new) * SCALE)
                total = total * old + jnp.sum(w, axis=1, keepdims=True)
                acc = acc * old + mix(w, keys_of(vf, j))
                return new, total, acc

            top, total, acc = lax.fori_loop(0, i, step, (top, total, acc))
            pos = (2 * i + core) * ROWS + lax.broadcasted_iota(jnp.int32, (ROWS, HS), 0)
            os_self[i] = jnp.where(pos < seq_len, acc * (1.0 / total), 0.0).astype(BF16)

            @pl.when(k < 7)
            def _():
                b_copy(i, k).start()

            @pl.when(k == 7)
            def _():
                pltpu.make_async_copy(os_self.at[z], self_out.at[0, :, own], misc.at[10]).start()

            return carry

        lax.fori_loop(0, 8, block, 0)

    own_fwd = forwards(0)
    for c in loads[1:]:
        c.wait()
    encode(0)
    shift_queries()
    encode(1)
    for c in local_in:
        c.wait()
    for c in own_fwd:
        c.start()
    tables()
    encode(2)
    encode(3)
    cross(0)
    cross(1)
    for part in range(3):
        for off in z_order:
            z_arrivals(off)[part].wait_recv()
            if part == 0:
                forwards(off)[0].start()
            if part == 2:
                forwards(off)[1].start()
    cross(2)
    for off in range(8):
        for c in forward_arrivals(off):
            c.wait_recv()
    self_attend()
    cross(3)

    for hc in range(CHUNKS):
        for off in range(3):
            gg = mod(g + 3 - off, 4)
            remote(
                os[hc].at[off], o_in.at[pl.ds(4 * gg, 4), :, pl.ds(hc * PAIR, PAIR)],
                o_send.at[hc * 3 + off], o_recv.at[hc * 3 + off], x_dev(gg),
            ).wait_recv()
            remote(
                ss[hc].at[off], st_in.at[4 * gg + hc],
                t_send.at[hc * 3 + off], t_recv.at[hc * 3 + off], x_dev(gg),
            ).wait_recv()
        for c in o_local(hc):
            c.wait()
    turned = jnp.transpose(st_in[...].reshape(128, 256))
    for gg in range(4):
        part = turned if gg == 0 else pltpu.roll(turned, 128 - 32 * gg, 1)
        for r in range(CAP):
            stat[gg * CAP + r] = part[r * SPAN : (r + 1) * SPAN, :]
    of[ROWS + 56 : ROWS + 64, :] = jnp.zeros((8, WIDTH), F32)

    def combine(u):
        s0, s1 = req_tab[2 * u], req_tab[2 * u + 1]
        l0, l1 = stat[s0], stat[s1]
        top = jnp.maximum(l0, l1)
        w0, w1 = jnp.exp2(l0 - top), jnp.exp2(l1 - top)
        inv = 1.0 / (w0 + w1)
        w0, w1 = w0 * inv, w1 * inv
        o0, o1 = o_in[s0], o_in[s1]
        first = SPAN - 1 + SPAN * u
        for h in range(8):
            lane = (h // 2) * 8 + h % 2
            at = slice(h * HS, (h + 1) * HS)
            of[first : first + SPAN, at] = (
                o0[:, at].astype(F32) * w0[:, lane : lane + 1]
                + o1[:, at].astype(F32) * w1[:, lane : lane + 1]
            )

    combine(3)
    tail_s[...] = of[ROWS : ROWS + SPAN, :].astype(BF16)
    tail_copy = remote(tail_s, tail_in, h_send.at[1], h_recv.at[1], ahead)
    tail_copy.start()
    for u in range(3):
        combine(u)
    first_pos = s * ROWS

    def live(first, rows):
        pos = first_pos + first + lax.broadcasted_iota(jnp.int32, (rows, WIDTH), 0)
        return jnp.logical_and(pos >= SPAN - 1, pos < seq_len)

    co[SPAN:ROWS, :] = jnp.where(live(SPAN, ROWS - SPAN), of[SPAN:ROWS, :], 0.0).astype(BF16)
    tail_copy.wait_recv()
    row = lax.broadcasted_iota(jnp.int32, (SPAN, WIDTH), 0)
    head = jnp.where(row < SPAN - 1, tail_in[...].astype(F32), of[0:SPAN, :])
    co[0:SPAN, :] = jnp.where(live(0, SPAN), head, 0.0).astype(BF16)
    out_copy = pltpu.make_async_copy(co, cross_out.at[0], misc.at[11])
    out_copy.start()

    pltpu.make_async_copy(os_self.at[z], self_out.at[0, :, own], misc.at[10]).wait()
    for k in range(7):
        src = mod(z + 7 - k, 8)
        cols = pl.ds(pl.multiple_of(src * HS, HS), HS)
        remote(
            os_self.at[z], self_out.at[0, :, cols], b_send.at[k], b_recv.at[k], z_dev(src)
        ).wait_recv()
        b_copy(mod(z + 1 + k, 8), k).wait_send()
    halo_copy.wait_send()
    tail_copy.wait_send()
    for c in idx_copies:
        c.wait_send()
    for off in z_order:
        for c in z_copies(off):
            c.wait_send()
    for off in range(8):
        for c in forwards(off):
            c.wait_send()
    for hc in range(CHUNKS):
        for off in range(3):
            y_copy(hc, off).wait_send()
            q_copy(hc, off).wait_send()
            o_copy(hc, off).wait_send()
            t_copy(hc, off).wait_send()
    out_copy.wait()


def local(*args):
    dec_query, dec_key, dec_value, cross_query, enc_query, enc_key, enc_value, nbr_index, seq_lengths = args
    any_ = pl.BlockSpec(memory_space=pl.ANY)
    smem = pl.BlockSpec(memory_space=pltpu.SMEM)
    V = pltpu.VMEM
    dma = lambda n: pltpu.SemaphoreType.DMA((n,))
    scratch = [V((2, 128, 4096), BF16)] * 3
    scratch += [V((ROWS, WIDTH), BF16), V((SPAN, WIDTH), BF16), V((ROWS + SPAN, WIDTH), F32)]
    scratch += [V((4, 2, 2, 128, PAIR), BF16)] * 4
    scratch += [V((8, 2, 128, PAIR), BF16)] * 4
    scratch += [V((16, SPAN, PAIR), BF16)] * 4
    scratch += [V((4, 4, SPAN, PAIR), BF16)] * 4
    scratch += [V((4, 8, 256), F32)] * 4
    scratch += [
        V((256, 128), F32), V((16, SPAN, WIDTH), BF16), V((16, 8, 256), F32),
        V((16, SPAN, 128), F32), V((ROWS + SPAN, WIDTH), F32),
        V((SPAN, WIDTH), BF16), V((SPAN, WIDTH), BF16), V((ROWS, WIDTH), BF16),
    ]
    scratch += [
        V((8, ROWS, HS), BF16), V((16, ROWS, HS), BF16), V((16, ROWS, HS), BF16), V((8, ROWS, HS), BF16)
    ]
    scratch += [
        V((8, 128), jnp.int32), V((4, 8, 128), jnp.int32), pltpu.SMEM((4, 8, 128), jnp.int32),
        pltpu.SMEM((16,), jnp.int32), pltpu.SMEM((16,), jnp.int32), pltpu.SMEM((8,), jnp.int32),
    ]
    scratch += [dma(n) for n in (7, 21, 21, 16, 16, 12, 12, 4, 12, 12, 12, 12, 12, 12, 3, 3, 7, 7, 2, 2, 12)]
    shape = jax.ShapeDtypeStruct((1, ROWS, WIDTH), BF16)
    return pl.pallas_call(
        kernel,
        out_shape=(shape, shape),
        in_specs=[smem, smem] + [any_] * 7,
        out_specs=(any_, any_),
        scratch_shapes=scratch,
        compiler_params=pltpu.CompilerParams(
            collective_id=0, has_side_effects=True, vmem_limit_bytes=56 << 20
        ),
        name="retro_block",
    )(nbr_index, seq_lengths, dec_query, dec_key, dec_value, cross_query, enc_query, enc_key, enc_value)


def solution(mesh):
    rows = P("grp", "seq", "mp")
    store = P(("grp", "seq", "mp"), None, None)
    return jax.shard_map(
        local,
        mesh=mesh,
        in_specs=(rows, rows, rows, rows, store, store, store, P("grp", "seq", None), P("grp")),
        out_specs=(rows, rows),
        check_vma=False,
    )
```

time: 352 us -> 101 us (0.29)
  the two profiles are of different devices: /device:TPU:1 before, /device:TPU:2 now
where the time goes in v1:
time: 101 us
  Pallas kernels  94.6 us (94%)
  local copies, waits for them, and re-layouts  5.07 us (5%)
  between operations  1.29 us (1%)
    pallas_call x1, Pallas kernels, local(): pl.pallas_call(kernel, out_shape=(shape, shape), in_specs=[smem, smem] +...  94.6 us
    unnamed x3, local copies, waits for them, and re-layouts  5.07 us

profile of v1, /device:TPU:2, one launch (start us, length us, event | category | flops | bytes accessed | tf_op | source)
XLA Modules:
  0.0 101.0 jit_solution(4768733303956558229)
XLA Ops:
  1.3 1.3 %copy.11.nbr = s32[1,4,2]{2,1,0:T(4,128)} copy(s32[1,4,2]{1,2,0:T(2,128)} %param.16) | data formatting | bytes 64 | tf_op args[7]
  2.6 94.6 %retro_block.1 = (bf16[1,256,1024]{2,1,0:T(8,128)(2,1)}, bf16[1,256,1024]{2,1,0:T(8,128)(2,1)}) custom-call(s32[1,4,2]{2,1,0:T(4,128)} %copy.11.nbr, s32[1]{0:T(128)S(6)} %copy.14.lens, bf16[1,256,1024]{2,1,0:T(8,128)(2,1)} %dq.1, bf16[1,256,1024]{2,1,0:T(8,128)(2,1)} %dk.1, bf16[1,256,1024]{2,1,0:T(8,128)(2,1)} %dv.1, bf16[1,256,1024]{2,1,0:T(8,128)(2,1)} %cq.1, ...), custom_call_target="tpu_custom_call" | custom-call | tf_op jit(solution)/shard_map/retro_block/pallas_call | solution.py:532
  97.2 1.9 %copy.15 = bf16[1,256,1024]{2,1,0:T(8,128)(2,1)} copy(bf16[1,256,1024]{2,1,0:T(8,128)(2,1)} %get-tuple-element.4) | data formatting | bytes 1048576
  99.1 1.9 %copy.16 = bf16[1,256,1024]{2,1,0:T(8,128)(2,1)} copy(bf16[1,256,1024]{2,1,0:T(8,128)(2,1)} %get-tuple-element.5) | data formatting | bytes 1048576

commit v2 on v1

v2 whole, which is shorter than its diff:
```python
import functools
import math

import jax
import jax.numpy as jnp
from jax import lax
from jax.experimental import pallas as pl
from jax.experimental.pallas import tpu as pltpu
from jax.sharding import PartitionSpec as P

HS = 128
SPAN = 64
CAP = 4
HEADS_OF = (2, 2, 2, 1, 1)
FIRST = (0, 2, 4, 6, 7)
CHUNKS = len(HEADS_OF)
ROWS = 256
WIDTH = 1024
SCALE = HS ** (-0.5) * math.log2(math.e)
MASKED = -1e30
MESH = pl.DeviceIdType.MESH
F32 = jnp.float32
BF16 = jnp.bfloat16
NT = (((1,), (1,)), ((), ()))


def mod(a, n):
    return lax.rem(a, n)


def scores_of(q, k):
    return lax.dot_general(q, k, NT, preferred_element_type=F32)


def mix(weights, v):
    return jnp.dot(weights.astype(BF16), v, preferred_element_type=F32)


def fold(x, op):
    parts = [x[:, a : a + HS] for a in range(0, x.shape[1], HS)]
    while len(parts) > 1:
        parts = [op(parts[a], parts[a + 1]) for a in range(0, len(parts), 2)]
    return parts[0]


def attend_all(queries, keys, values):
    scores = [scores_of(q, k) for q, k in zip(queries, keys)]
    tops = [jnp.max(x, axis=1, keepdims=True) for x in scores]
    weights = [jnp.exp2((x - top) * SCALE) for x, top in zip(scores, tops)]
    totals = [jnp.sum(w, axis=1, keepdims=True) for w in weights]
    sums = [mix(w, v) for w, v in zip(weights, values)]
    return tops, totals, [x * (1.0 / total) for x, total in zip(sums, totals)]


def kernel(
    nbr, lens, dq, dk, dv, cq, eq, ek, ev,
    self_out, cross_out,
    eqv, ekv, evv, cqv, halo, qf,
    stage, stat, of, co,
    qs, kf, vf, os_self, sc_buf,
    idx_s, idx_all, idx_sm, row_tab, id_tab, req_tab,
    load_sem, z_send, z_recv, f_send, f_recv, y_send, y_recv, y_loc,
    q_send, q_recv, o_send, o_recv, t_send, t_recv, o_loc, t_loc, i_send, i_recv,
    b_send, b_recv, h_send, h_recv, e_send, e_recv, c_sem, misc,
    *chunked,
):
    kvs, pool, qb, os, ss, o_in, st_in, tail_s, tail_in = (
        chunked[n * CHUNKS : (n + 1) * CHUNKS] for n in range(9)
    )
    g = lax.axis_index("grp")
    s = lax.axis_index("seq")
    m = lax.axis_index("mp")
    z = lax.div(s, 2)
    core = lax.rem(s, 2)
    seq_len = lens[0]

    def z_dev(zz):
        return (g, 2 * zz + core, m)

    def y_dev(mm):
        return (g, s, mm)

    def x_dev(gg):
        return (gg, s, m)

    partner = (g, s + 1 - 2 * core, m)
    other = (g, mod(s + 15 + 2 * core, 16), m)
    behind = (g, mod(s + 15, 16), m)
    ahead = (g, mod(s + 1, 16), m)

    def remote(src, dst, send, recv, dev):
        return pltpu.make_async_remote_copy(
            src_ref=src, dst_ref=dst, send_sem=send, recv_sem=recv,
            device_id=dev, device_id_type=MESH,
        )

    loads = [
        pltpu.make_async_copy(src, dst, load_sem.at[n])
        for n, (src, dst) in enumerate(((cq.at[0], cqv), (eq, eqv), (ek, ekv), (ev, evv)))
    ]
    for c in loads:
        c.start()
    own = pl.ds(pl.multiple_of(z * HS, HS), HS)
    local_in = [
        pltpu.make_async_copy(dq.at[0, :, own], qs.at[z], load_sem.at[4]),
        pltpu.make_async_copy(dk.at[0, :, own], kf.at[s], load_sem.at[5]),
        pltpu.make_async_copy(dv.at[0, :, own], vf.at[s], load_sem.at[6]),
    ]
    for c in local_in:
        c.start()

    bar = pltpu.get_barrier_semaphore()
    peers = [z_dev(mod(z + off, 8)) for off in range(1, 8)]
    peers += [y_dev(mod(m + off, 4)) for off in range(1, 4)]
    peers += [x_dev(mod(g + off, 4)) for off in range(1, 4)]
    peers += [partner, other]
    for dev in peers:
        pl.semaphore_signal(bar, inc=1, device_id=dev, device_id_type=MESH)
    pl.semaphore_wait(bar, len(peers))

    halo_copy = remote(cq.at[0, pl.ds(0, SPAN)], halo, h_send.at[0], h_recv.at[0], behind)
    halo_copy.start()

    lane8 = lax.broadcasted_iota(jnp.int32, (8, 128), 1)
    packed = jnp.zeros((8, 128), jnp.int32)
    for n in range(8):
        packed = jnp.where(lane8 == n, nbr[0, n % 2, n // 2], packed)
    idx_s[...] = packed
    idx_copies = [
        remote(idx_s, idx_all.at[g], i_send.at[off - 1], i_recv.at[off - 1], x_dev(mod(g + off, 4)))
        for off in range(1, 4)
    ]
    for c in idx_copies:
        c.start()
    idx_local = pltpu.make_async_copy(idx_s, idx_all.at[g], misc.at[0])
    idx_local.start()

    z_order = (4, 3, 5, 2, 6, 1, 7)

    def z_copy(off, part):
        zz = mod(z + off, 8)
        cols = pl.ds(pl.multiple_of(zz * HS, HS), HS)
        src = (dk, dq, dv)[part].at[0, :, cols]
        dst = (kf.at[s], qs.at[z], vf.at[s])[part]
        n = (off - 1) * 3 + part
        return remote(src, dst, z_send.at[n], z_recv.at[n], z_dev(zz))

    def z_arrival(off, part):
        zz = mod(z + 8 - off, 8)
        b = 2 * zz + core
        dst = (kf.at[b], qs.at[zz], vf.at[b])[part]
        n = (off - 1) * 3 + part
        return remote(dst, dst, z_send.at[n], z_recv.at[n], z_dev(zz))

    def forward(off, part):
        ref = (kf, vf)[part].at[2 * mod(z + 8 - off, 8) + core]
        n = off * 2 + part
        return remote(ref, ref, f_send.at[n], f_recv.at[n], partner)

    def forward_arrival(off, part):
        ref = (kf, vf)[part].at[2 * mod(z + 8 - off, 8) + 1 - core]
        n = off * 2 + part
        return remote(ref, ref, f_send.at[n], f_recv.at[n], partner)

    for part in range(3):
        for off in z_order:
            z_copy(off, part).start()

    def columns(hc):
        return slice(FIRST[hc] * HS, (FIRST[hc] + HEADS_OF[hc]) * HS)

    def y_copy(hc, off):
        return remote(
            kvs[hc].at[off], pool[hc].at[pl.ds(2 * m, 2)],
            y_send.at[hc * 3 + off], y_recv.at[hc * 3 + off], y_dev(mod(m + 1 + off, 4)),
        )

    def y_arrival(hc, off):
        mm = mod(m + 3 - off, 4)
        return remote(
            kvs[hc].at[off], pool[hc].at[pl.ds(2 * mm, 2)],
            y_send.at[hc * 3 + off], y_recv.at[hc * 3 + off], y_dev(mm),
        )

    def y_local(hc):
        return pltpu.make_async_copy(kvs[hc].at[3], pool[hc].at[pl.ds(2 * m, 2)], y_loc.at[hc])

    def encode(hc):
        out = kvs[hc]

        def step(off, carry):
            t = mod(m + 1 + off, 4)
            tiles = [(n, j) for n in range(2) for j in range(HEADS_OF[hc])]
            cols = [
                pl.ds(pl.multiple_of((t * 8 + FIRST[hc] + j) * HS, HS), HS) for n, j in tiles
            ]
            q = [eqv[n, :, c] for (n, j), c in zip(tiles, cols)]
            k = [ekv[n, :, c] for (n, j), c in zip(tiles, cols)]
            v = [evv[n, :, c] for (n, j), c in zip(tiles, cols)]
            _, _, mixed = attend_all(q, k, v)
            for a, (n, j) in enumerate(tiles):
                at = slice(j * HS, (j + 1) * HS)
                out[off, n, 0, :, at] = (k[a].astype(F32) + mixed[a]).astype(BF16)
                out[off, n, 1, :, at] = (v[a].astype(F32) + mixed[a]).astype(BF16)

            @pl.when(off < 3)
            def _():
                y_copy(hc, off).start()

            @pl.when(off == 3)
            def _():
                y_local(hc).start()

            return carry

        lax.fori_loop(0, 4, step, 0)

    def q_copy(hc, off):
        mine = qb[hc].at[pl.ds(4 * g, 4)]
        return remote(
            mine, mine, q_send.at[hc * 3 + off], q_recv.at[hc * 3 + off], x_dev(mod(g + 1 + off, 4))
        )

    def q_arrival(hc, off):
        gg = mod(g + 3 - off, 4)
        theirs = qb[hc].at[pl.ds(4 * gg, 4)]
        return remote(
            theirs, theirs, q_send.at[hc * 3 + off], q_recv.at[hc * 3 + off], x_dev(gg)
        )

    def shift_queries():
        loads[0].wait()
        halo_copy.wait_recv()
        qf[0:ROWS, :] = cqv[...].astype(F32)
        qf[ROWS : ROWS + SPAN, :] = halo[...].astype(F32)
        for hc in range(CHUNKS):
            for u in range(4):
                first = SPAN - 1 + SPAN * u
                qb[hc][4 * g + u] = qf[first : first + SPAN, columns(hc)].astype(BF16)
            for off in range(3):
                q_copy(hc, off).start()

    def tables():
        for off in range(1, 4):
            gg = mod(g + 4 - off, 4)
            remote(
                idx_s, idx_all.at[gg], i_send.at[off - 1], i_recv.at[off - 1], x_dev(gg)
            ).wait_recv()
        idx_local.wait()
        to_smem = pltpu.make_async_copy(idx_all, idx_sm, misc.at[1])
        to_smem.start()
        to_smem.wait()

        def per_candidate(c, carry):
            ids = [idx_sm[c, 0, n] for n in range(8)]
            count = jnp.int32(0)
            rows = [c * 4] * CAP
            locals_ = [jnp.int32(0)] * CAP
            for n in range(8):
                mine = lax.shift_right_logical(ids[n], 7) == g
                for r in range(CAP):
                    hit = jnp.logical_and(mine, count == r)
                    rows[r] = jnp.where(hit, c * 4 + n // 2, rows[r])
                    locals_[r] = jnp.where(hit, ids[n] & 7, locals_[r])
                count = count + jnp.where(mine, 1, 0)
            for r in range(CAP):
                row_tab[c * 4 + r] = rows[r]
                id_tab[c * 4 + r] = locals_[r]
            return carry

        lax.fori_loop(0, 4, per_candidate, 0)
        targets = [lax.shift_right_logical(nbr[0, n % 2, n // 2], 7) for n in range(8)]
        for n in range(8):
            rank = jnp.int32(0)
            for e in range(n):
                rank = rank + jnp.where(targets[e] == targets[n], 1, 0)
            req_tab[n] = targets[n] * CAP + rank

    lane64 = lax.broadcasted_iota(jnp.int32, (SPAN, 128), 1)

    def o_copy(hc, off):
        return remote(
            os[hc].at[off], o_in[hc].at[pl.ds(4 * g, 4)],
            o_send.at[hc * 3 + off], o_recv.at[hc * 3 + off], x_dev(mod(g + 1 + off, 4)),
        )

    def t_copy(hc, off):
        return remote(
            ss[hc].at[off], st_in[hc].at[g],
            t_send.at[hc * 3 + off], t_recv.at[hc * 3 + off], x_dev(mod(g + 1 + off, 4)),
        )

    def o_local(hc):
        return (
            pltpu.make_async_copy(
                os[hc].at[3], o_in[hc].at[pl.ds(4 * g, 4)], o_loc.at[hc]
            ),
            pltpu.make_async_copy(ss[hc].at[3], st_in[hc].at[g], t_loc.at[hc]),
        )

    def cross(hc):
        for off in range(3):
            y_arrival(hc, off).wait_recv()
            q_arrival(hc, off).wait_recv()
        y_local(hc).wait()

        def step(off, carry):
            c = mod(g + 1 + off, 4)
            heads = range(HEADS_OF[hc])
            tiles = [(r, j) for r in range(CAP) for j in heads]
            q2 = [qb[hc][row_tab[c * 4 + r]] for r in range(CAP)]
            k2 = [pool[hc][id_tab[c * 4 + r], 0] for r in range(CAP)]
            v2 = [pool[hc][id_tab[c * 4 + r], 1] for r in range(CAP)]

            def split(x):
                return [x[r][:, j * HS : (j + 1) * HS] for r, j in tiles]

            tops, totals, mixed = attend_all(split(q2), split(k2), split(v2))
            logs = [top * SCALE + jnp.log2(total) for top, total in zip(tops, totals)]
            for a, (r, j) in enumerate(tiles):
                os[hc][off, r, :, j * HS : (j + 1) * HS] = mixed[a].astype(BF16)
            for r in range(CAP):
                row = jnp.where(lane64 == 0, logs[r * len(heads)], 0.0)
                for j in heads[1:]:
                    row = jnp.where(lane64 == j, logs[r * len(heads) + j], row)
                stage[r * SPAN : (r + 1) * SPAN, :] = row
            ss[hc][off] = jnp.transpose(stage[...])[0:8]

            @pl.when(off < 3)
            def _():
                o_copy(hc, off).start()
                t_copy(hc, off).start()

            @pl.when(off == 3)
            def _():
                for c_ in o_local(hc):
                    c_.start()

            return carry

        lax.fori_loop(0, 4, step, 0)

    def b_copy(i, k):
        return remote(
            os_self.at[i], self_out.at[0, :, own], b_send.at[k], b_recv.at[k], z_dev(i)
        )

    KEYS = 512
    key_iota = lax.broadcasted_iota(jnp.int32, (ROWS, KEYS), 1)
    row_iota = lax.broadcasted_iota(jnp.int32, (ROWS, KEYS), 0)

    def self_attend():
        for n, i in enumerate(reversed(range(8))):
            q = qs[i]
            top = None
            for j in range(i + 1):
                sc = scores_of(q, kf[2 * j : 2 * j + 2].reshape(KEYS, HS))
                if j == i:
                    sc = jnp.where(key_iota <= row_iota + core * ROWS, sc, MASKED)
                sc_buf[j] = sc
                high = fold(sc, jnp.maximum)
                top = high if top is None else jnp.maximum(top, high)
            top = jnp.max(top, axis=1, keepdims=True) * SCALE
            if n == 0:
                for off in range(8):
                    forward_arrival(off, 1).wait_recv()
            total = acc = None
            for j in range(i + 1):
                w = jnp.exp2(sc_buf[j] * SCALE - top)
                low = fold(w, jnp.add)
                part = mix(w, vf[2 * j : 2 * j + 2].reshape(KEYS, HS))
                total, acc = (low, part) if total is None else (total + low, acc + part)
            total = jnp.sum(total, axis=1, keepdims=True)
            pos = (2 * i + core) * ROWS + lax.broadcasted_iota(jnp.int32, (ROWS, HS), 0)
            os_self[i] = jnp.where(pos < seq_len, acc * (1.0 / total), 0.0).astype(BF16)
        for k in (3, 2, 4, 1, 5, 0, 6):
            b_copy(mod(z + 1 + k, 8), k).start()
        pltpu.make_async_copy(os_self.at[z], self_out.at[0, :, own], misc.at[10]).start()

    first_pos = s * ROWS

    def o_arrivals(hc):
        for off in range(3):
            gg = mod(g + 3 - off, 4)
            n = hc * 3 + off
            remote(
                os[hc].at[off], o_in[hc].at[pl.ds(4 * gg, 4)], o_send.at[n], o_recv.at[n], x_dev(gg)
            ).wait_recv()
            remote(
                ss[hc].at[off], st_in[hc].at[gg], t_send.at[n], t_recv.at[n], x_dev(gg)
            ).wait_recv()
        for c in o_local(hc):
            c.wait()

    def tail_copy(hc):
        return remote(tail_s[hc], tail_in[hc], e_send.at[hc], e_recv.at[hc], ahead)

    def out_copy(hc):
        return pltpu.make_async_copy(
            co.at[:, columns(hc)], cross_out.at[0, :, columns(hc)], c_sem.at[hc]
        )

    def live(first, rows, width):
        pos = first_pos + first + lax.broadcasted_iota(jnp.int32, (rows, width), 0)
        return jnp.logical_and(pos >= SPAN - 1, pos < seq_len)

    def combine(hc):
        width = HEADS_OF[hc] * HS
        cols = columns(hc)
        o_arrivals(hc)
        logs = jnp.concatenate([st_in[hc][...].reshape(32, 256), jnp.zeros((96, 256), F32)], axis=0)
        turned = jnp.transpose(logs)
        for gg in range(4):
            part = turned if gg == 0 else pltpu.roll(turned, 128 - 8 * gg, 1)
            for r in range(CAP):
                stat[gg * CAP + r] = part[r * SPAN : (r + 1) * SPAN, :]
        of[ROWS + 56 : ROWS + 64, cols] = jnp.zeros((8, width), F32)
        for u in (3, 0, 1, 2):
            s0, s1 = req_tab[2 * u], req_tab[2 * u + 1]
            l0, l1 = stat[s0], stat[s1]
            top = jnp.maximum(l0, l1)
            w0, w1 = jnp.exp2(l0 - top), jnp.exp2(l1 - top)
            inv = 1.0 / (w0 + w1)
            w0, w1 = w0 * inv, w1 * inv
            o0, o1 = o_in[hc][s0], o_in[hc][s1]
            first = SPAN - 1 + SPAN * u
            for j in range(HEADS_OF[hc]):
                at = slice(j * HS, (j + 1) * HS)
                of[first : first + SPAN, cols.start + j * HS : cols.start + (j + 1) * HS] = (
                    o0[:, at].astype(F32) * w0[:, j : j + 1]
                    + o1[:, at].astype(F32) * w1[:, j : j + 1]
                )
            if u == 3:
                tail_s[hc][...] = of[ROWS : ROWS + SPAN, cols].astype(BF16)
                tail_copy(hc).start()
        co[SPAN:ROWS, cols] = jnp.where(
            live(SPAN, ROWS - SPAN, width), of[SPAN:ROWS, cols], 0.0
        ).astype(BF16)

    def finish(hc):
        width = HEADS_OF[hc] * HS
        cols = columns(hc)
        tail_copy(hc).wait_recv()
        row = lax.broadcasted_iota(jnp.int32, (SPAN, width), 0)
        head = jnp.where(row < SPAN - 1, tail_in[hc][...].astype(F32), of[0:SPAN, cols])
        co[0:SPAN, cols] = jnp.where(live(0, SPAN, width), head, 0.0).astype(BF16)
        out_copy(hc).start()

    for c in loads[1:]:
        c.wait()
    encode(0)
    shift_queries()
    for hc in range(1, CHUNKS):
        encode(hc)
    for c in local_in:
        c.wait()
    for part in range(2):
        forward(0, part).start()
    tables()
    cross(0)
    for off in z_order:
        z_arrival(off, 0).wait_recv()
        forward(off, 0).start()
    cross(1)
    for off in z_order:
        z_arrival(off, 1).wait_recv()
    cross(2)
    for off in z_order:
        z_arrival(off, 2).wait_recv()
        forward(off, 1).start()
    for off in range(8):
        forward_arrival(off, 0).wait_recv()
    self_attend()
    cross(3)
    combine(0)
    combine(1)
    cross(4)
    combine(2)
    combine(3)
    for hc in range(3):
        finish(hc)
    combine(4)
    finish(3)
    finish(4)

    pltpu.make_async_copy(os_self.at[z], self_out.at[0, :, own], misc.at[10]).wait()
    for k in range(7):
        src = mod(z + 7 - k, 8)
        cols = pl.ds(pl.multiple_of(src * HS, HS), HS)
        remote(
            os_self.at[z], self_out.at[0, :, cols], b_send.at[k], b_recv.at[k], z_dev(src)
        ).wait_recv()
        b_copy(mod(z + 1 + k, 8), k).wait_send()
    halo_copy.wait_send()
    for c in idx_copies:
        c.wait_send()
    for part in range(3):
        for off in z_order:
            z_copy(off, part).wait_send()
    for off in range(8):
        for part in range(2):
            forward(off, part).wait_send()
    for hc in range(CHUNKS):
        for off in range(3):
            y_copy(hc, off).wait_send()
            q_copy(hc, off).wait_send()
            o_copy(hc, off).wait_send()
            t_copy(hc, off).wait_send()
        tail_copy(hc).wait_send()
        out_copy(hc).wait()


def local(*args):
    dec_query, dec_key, dec_value, cross_query, enc_query, enc_key, enc_value, nbr_index, seq_lengths = args
    any_ = pl.BlockSpec(memory_space=pl.ANY)
    smem = pl.BlockSpec(memory_space=pltpu.SMEM)
    V = pltpu.VMEM
    dma = lambda n: pltpu.SemaphoreType.DMA((n,))
    scratch = [V((2, 128, 4096), BF16)] * 3
    scratch += [V((ROWS, WIDTH), BF16), V((SPAN, WIDTH), BF16), V((ROWS + SPAN, WIDTH), F32)]
    scratch += [
        V((256, 128), F32), V((16, SPAN, 128), F32), V((ROWS + SPAN, WIDTH), F32),
        V((ROWS, WIDTH), BF16),
    ]
    scratch += [
        V((8, ROWS, HS), BF16), V((16, ROWS, HS), BF16), V((16, ROWS, HS), BF16),
        V((8, ROWS, HS), BF16), V((8, ROWS, 512), F32),
    ]
    scratch += [
        V((8, 128), jnp.int32), V((4, 8, 128), jnp.int32), pltpu.SMEM((4, 8, 128), jnp.int32),
        pltpu.SMEM((16,), jnp.int32), pltpu.SMEM((16,), jnp.int32), pltpu.SMEM((8,), jnp.int32),
    ]
    per = 3 * CHUNKS
    scratch += [
        dma(n)
        for n in (
            7, 21, 21, 16, 16, per, per, CHUNKS, per, per, per, per, per, per, CHUNKS, CHUNKS,
            3, 3, 7, 7, 1, 1, CHUNKS, CHUNKS, CHUNKS, 12,
        )
    ]
    widths = [n * HS for n in HEADS_OF]
    for form in (
        lambda w: V((4, 2, 2, 128, w), BF16),
        lambda w: V((8, 2, 128, w), BF16),
        lambda w: V((16, SPAN, w), BF16),
        lambda w: V((4, 4, SPAN, w), BF16),
        lambda w: V((4, 8, 256), F32),
        lambda w: V((16, SPAN, w), BF16),
        lambda w: V((4, 8, 256), F32),
        lambda w: V((SPAN, w), BF16),
        lambda w: V((SPAN, w), BF16),
    ):
        scratch += [form(w) for w in widths]
    shape = jax.ShapeDtypeStruct((1, ROWS, WIDTH), BF16)
    return pl.pallas_call(
        kernel,
        out_shape=(shape, shape),
        in_specs=[smem, smem] + [any_] * 7,
        out_specs=(any_, any_),
        scratch_shapes=scratch,
        compiler_params=pltpu.CompilerParams(
            collective_id=0, has_side_effects=True, vmem_limit_bytes=56 << 20
        ),
        name="retro_block",
    )(jnp.transpose(nbr_index, (0, 2, 1)), seq_lengths, dec_query, dec_key, dec_value, cross_query, enc_query, enc_key, enc_value)


def solution(mesh):
    rows = P("grp", "seq", "mp")
    store = P(("grp", "seq", "mp"), None, None)
    return jax.shard_map(
        local,
        mesh=mesh,
        in_specs=(rows, rows, rows, rows, store, store, store, P("grp", "seq", None), P("grp")),
        out_specs=(rows, rows),
        check_vma=False,
    )
```

time: 101 us -> 83.6 us (0.83)
  the two profiles are of different devices: /device:TPU:2 before, /device:TPU:1 now
where the time goes in v2:
time: 83.6 us; the launch traced here: 83.4 us
  Pallas kernels  78.3 us (94%)
  local copies, waits for them, and re-layouts  3.74 us (4%)
  between operations  1.29 us (2%)
    pallas_call x1, Pallas kernels, local(): pl.pallas_call(kernel, out_shape=(shape, shape), in_specs=[smem, smem] +...  78.3 us
    unnamed x2, local copies, waits for them, and re-layouts  3.74 us

profile of v2, /device:TPU:1, one launch (start us, length us, event | category | flops | bytes accessed | tf_op | source)
XLA Modules:
  0.0 83.4 jit_solution(3941687574234828413)
XLA Ops:
  1.3 78.3 %retro_block.1 = (bf16[1,256,1024]{2,1,0:T(8,128)(2,1)}, bf16[1,256,1024]{2,1,0:T(8,128)(2,1)}) custom-call(s32[1,2,4]{2,1,0:T(2,128)} %bitcast.1, s32[1]{0:T(128)S(6)} %copy.13.lens, bf16[1,256,1024]{2,1,0:T(8,128)(2,1)} %dq.1, bf16[1,256,1024]{2,1,0:T(8,128)(2,1)} %dk.1, bf16[1,256,1024]{2,1,0:T(8,128)(2,1)} %dv.1, bf16[1,256,1024]{2,1,0:T(8,128)(2,1)} %cq.1, ...), custom_call_target="tpu_custom_call" | custom-call | tf_op jit(solution)/shard_map/retro_block/pallas_call | solution.py:555
  79.6 1.9 %copy.14 = bf16[1,256,1024]{2,1,0:T(8,128)(2,1)} copy(bf16[1,256,1024]{2,1,0:T(8,128)(2,1)} %get-tuple-element.4) | data formatting | bytes 1048576
  81.5 1.9 %copy.15 = bf16[1,256,1024]{2,1,0:T(8,128)(2,1)} copy(bf16[1,256,1024]{2,1,0:T(8,128)(2,1)} %get-tuple-element.5) | data formatting | bytes 1048576

commit v3 on v2

--- a/solution.py
+++ b/solution.py
@@ -11,8 +11,8 @@
 HS = 128
 SPAN = 64
 CAP = 4
-HEADS_OF = (2, 2, 2, 1, 1)
-FIRST = (0, 2, 4, 6, 7)
+HEADS_OF = (1, 2, 2, 2, 1)
+FIRST = (0, 1, 3, 5, 7)
 CHUNKS = len(HEADS_OF)
 ROWS = 256
 WIDTH = 1024
@@ -57,7 +57,7 @@
     self_out, cross_out,
     eqv, ekv, evv, cqv, halo, qf,
     stage, stat, of, co,
-    qs, kf, vf, os_self, sc_buf,
+    qs, kf, vf, os_self, sc_buf, p_buf, tot_buf,
     idx_s, idx_all, idx_sm, row_tab, id_tab, req_tab,
     load_sem, z_send, z_recv, f_send, f_recv, y_send, y_recv, y_loc,
     q_send, q_recv, o_send, o_recv, t_send, t_recv, o_loc, t_loc, i_send, i_recv,
@@ -349,8 +349,8 @@
     key_iota = lax.broadcasted_iota(jnp.int32, (ROWS, KEYS), 1)
     row_iota = lax.broadcasted_iota(jnp.int32, (ROWS, KEYS), 0)
 
-    def self_attend():
-        for n, i in enumerate(reversed(range(8))):
+    def self_weights():
+        for i in reversed(range(8)):
             q = qs[i]
             top = None
             for j in range(i + 1):
@@ -361,16 +361,22 @@
                 high = fold(sc, jnp.maximum)
                 top = high if top is None else jnp.maximum(top, high)
             top = jnp.max(top, axis=1, keepdims=True) * SCALE
-            if n == 0:
-                for off in range(8):
-                    forward_arrival(off, 1).wait_recv()
-            total = acc = None
+            total = None
             for j in range(i + 1):
                 w = jnp.exp2(sc_buf[j] * SCALE - top)
+                p_buf[i, :, j * KEYS : (j + 1) * KEYS] = w.astype(BF16)
                 low = fold(w, jnp.add)
-                part = mix(w, vf[2 * j : 2 * j + 2].reshape(KEYS, HS))
-                total, acc = (low, part) if total is None else (total + low, acc + part)
-            total = jnp.sum(total, axis=1, keepdims=True)
+                total = low if total is None else total + low
+            tot_buf[i] = total
+
+    def self_values():
+        for i in reversed(range(8)):
+            acc = jnp.dot(
+                p_buf[i, :, 0 : (i + 1) * KEYS],
+                vf[0 : 2 * i + 2].reshape((i + 1) * KEYS, HS),
+                preferred_element_type=F32,
+            )
+            total = jnp.sum(tot_buf[i], axis=1, keepdims=True)
             pos = (2 * i + core) * ROWS + lax.broadcasted_iota(jnp.int32, (ROWS, HS), 0)
             os_self[i] = jnp.where(pos < seq_len, acc * (1.0 / total), 0.0).astype(BF16)
         for k in (3, 2, 4, 1, 5, 0, 6):
@@ -446,6 +452,17 @@
         co[0:SPAN, cols] = jnp.where(live(0, SPAN, width), head, 0.0).astype(BF16)
         out_copy(hc).start()
 
+    def sent(hc):
+        for off in range(3):
+            y_copy(hc, off).wait_send()
+            q_copy(hc, off).wait_send()
+
+    def answered(hc):
+        for off in range(3):
+            o_copy(hc, off).wait_send()
+            t_copy(hc, off).wait_send()
+        tail_copy(hc).wait_send()
+
     for c in loads[1:]:
         c.wait()
     encode(0)
@@ -461,27 +478,50 @@
     for off in z_order:
         z_arrival(off, 0).wait_recv()
         forward(off, 0).start()
+    halo_copy.wait_send()
+    for c in idx_copies:
+        c.wait_send()
     cross(1)
+    sent(0)
     for off in z_order:
         z_arrival(off, 1).wait_recv()
+    for off in range(8):
+        forward_arrival(off, 0).wait_recv()
+    self_weights()
     cross(2)
     for off in z_order:
         z_arrival(off, 2).wait_recv()
         forward(off, 1).start()
+    sent(1)
+    for off in z_order:
+        for part in range(3):
+            z_copy(off, part).wait_send()
     for off in range(8):
-        forward_arrival(off, 0).wait_recv()
-    self_attend()
+        forward_arrival(off, 1).wait_recv()
+    self_values()
+    combine(0)
     cross(3)
-    combine(0)
     combine(1)
     cross(4)
+    sent(2)
+    sent(3)
+    sent(4)
+    for off in range(8):
+        for part in range(2):
+            forward(off, part).wait_send()
     combine(2)
+    finish(0)
+    finish(1)
     combine(3)
-    for hc in range(3):
-        finish(hc)
+    answered(0)
+    answered(1)
+    finish(2)
     combine(4)
     finish(3)
+    answered(2)
+    answered(3)
     finish(4)
+    answered(4)
 
     pltpu.make_async_copy(os_self.at[z], self_out.at[0, :, own], misc.at[10]).wait()
     for k in range(7):
@@ -491,23 +531,29 @@
             os_self.at[z], self_out.at[0, :, cols], b_send.at[k], b_recv.at[k], z_dev(src)
         ).wait_recv()
         b_copy(mod(z + 1 + k, 8), k).wait_send()
-    halo_copy.wait_send()
-    for c in idx_copies:
-        c.wait_send()
-    for part in range(3):
-        for off in z_order:
-            z_copy(off, part).wait_send()
-    for off in range(8):
-        for part in range(2):
-            forward(off, part).wait_send()
     for hc in range(CHUNKS):
-        for off in range(3):
-            y_copy(hc, off).wait_send()
-            q_copy(hc, off).wait_send()
-            o_copy(hc, off).wait_send()
-            t_copy(hc, off).wait_send()
-        tail_copy(hc).wait_send()
         out_copy(hc).wait()
+
+
+def place(a_ref, b_ref, a_out, b_out, held, in_sem, out_sem):
+    pieces = [
+        (src.at[0, pl.ds(half * 128, 128)], dst.at[0, pl.ds(half * 128, 128)])
+        for half in range(2)
+        for src, dst in ((a_ref, a_out), (b_ref, b_out))
+    ]
+    loads = [
+        pltpu.make_async_copy(src, held.at[n], in_sem.at[n]) for n, (src, _) in enumerate(pieces)
+    ]
+    stores = [
+        pltpu.make_async_copy(held.at[n], dst, out_sem.at[n]) for n, (_, dst) in enumerate(pieces)
+    ]
+    for c in loads:
+        c.start()
+    for load, store in zip(loads, stores):
+        load.wait()
+        store.start()
+    for c in stores:
+        c.wait()
 
 
 def local(*args):
@@ -524,7 +570,7 @@
     ]
     scratch += [
         V((8, ROWS, HS), BF16), V((16, ROWS, HS), BF16), V((16, ROWS, HS), BF16),
-        V((8, ROWS, HS), BF16), V((8, ROWS, 512), F32),
+        V((8, ROWS, HS), BF16), V((8, ROWS, 512), F32), V((8, ROWS, 4096), BF16), V((8, ROWS, HS), F32),
     ]
     scratch += [
         V((8, 128), jnp.int32), V((4, 8, 128), jnp.int32), pltpu.SMEM((4, 8, 128), jnp.int32),
@@ -552,7 +598,7 @@
     ):
         scratch += [form(w) for w in widths]
     shape = jax.ShapeDtypeStruct((1, ROWS, WIDTH), BF16)
-    return pl.pallas_call(
+    both = pl.pallas_call(
         kernel,
         out_shape=(shape, shape),
         in_specs=[smem, smem] + [any_] * 7,
@@ -563,6 +609,14 @@
         ),
         name="retro_block",
     )(jnp.transpose(nbr_index, (0, 2, 1)), seq_lengths, dec_query, dec_key, dec_value, cross_query, enc_query, enc_key, enc_value)
+    return pl.pallas_call(
+        place,
+        out_shape=(shape, shape),
+        in_specs=[any_] * 2,
+        out_specs=(any_, any_),
+        scratch_shapes=[V((4, 128, WIDTH), BF16), dma(4), dma(4)],
+        name="place",
+    )(*both)
 
 
 def solution(mesh):

time: 83.6 us -> 75.4 us (0.902)
  Pallas kernels: 78.3 us -> 74 us
  local copies, waits for them, and re-layouts: 3.74 us -> 0 us
    pallas_call x1, Pallas kernels: 78.3 us -> 72 us  [local(): pl.pallas_call(kernel, out_shape=(shape, shape), in_specs=[smem, smem] +...]
    unnamed x2 -> x0, local copies, waits for them, and re-layouts: 3.74 us -> none
    pallas_call x0 -> x1, Pallas kernels: none -> 1.98 us  [local(): pl.pallas_call(place, out_shape=(shape, shape), in_specs=[any_] * 2, out_...]
where the time goes in v3:
time: 75.4 us; the launch traced here: 75.2 us
  Pallas kernels  74 us (98%)
  between operations  1.29 us (2%)
    pallas_call x1, Pallas kernels, local(): pl.pallas_call(kernel, out_shape=(shape, shape), in_specs=[smem, smem] +...  72 us
    pallas_call x1, Pallas kernels, local(): pl.pallas_call(place, out_shape=(shape, shape), in_specs=[any_] * 2, out_...  1.98 us

profile of v3, /device:TPU:1, one launch (start us, length us, event | category | flops | bytes accessed | tf_op | source)
XLA Modules:
  0.0 75.2 jit_solution(12336002551597966532)
XLA Ops:
  1.3 72.0 %retro_block.1 = (bf16[1,256,1024]{2,1,0:T(8,128)(2,1)}, bf16[1,256,1024]{2,1,0:T(8,128)(2,1)}) custom-call(s32[1,2,4]{2,1,0:T(2,128)} %bitcast.1, s32[1]{0:T(128)S(6)} %copy.11.lens, bf16[1,256,1024]{2,1,0:T(8,128)(2,1)} %dq.1, bf16[1,256,1024]{2,1,0:T(8,128)(2,1)} %dk.1, bf16[1,256,1024]{2,1,0:T(8,128)(2,1)} %dv.1, bf16[1,256,1024]{2,1,0:T(8,128)(2,1)} %cq.1, ...), custom_call_target="tpu_custom_call" | custom-call | tf_op jit(solution)/shard_map/retro_block/pallas_call | solution.py:601
  73.3 2.0 %place.1 = (bf16[1,256,1024]{2,1,0:T(8,128)(2,1)}, bf16[1,256,1024]{2,1,0:T(8,128)(2,1)}) custom-call(bf16[1,256,1024]{2,1,0:T(8,128)(2,1)} %get-tuple-element.4.a_ref, bf16[1,256,1024]{2,1,0:T(8,128)(2,1)} %get-tuple-element.5.b_ref), custom_call_target="tpu_custom_call" | custom-call | tf_op jit(solution)/shard_map/place/pallas_call | solution.py:612

commit v4 on v3

--- a/solution.py
+++ b/solution.py
@@ -103,8 +103,8 @@
     own = pl.ds(pl.multiple_of(z * HS, HS), HS)
     local_in = [
         pltpu.make_async_copy(dq.at[0, :, own], qs.at[z], load_sem.at[4]),
-        pltpu.make_async_copy(dk.at[0, :, own], kf.at[s], load_sem.at[5]),
-        pltpu.make_async_copy(dv.at[0, :, own], vf.at[s], load_sem.at[6]),
+        pltpu.make_async_copy(dk.at[0, :, own], kf.at[core, z], load_sem.at[5]),
+        pltpu.make_async_copy(dv.at[0, :, own], vf.at[core, z], load_sem.at[6]),
     ]
     for c in local_in:
         c.start()
@@ -127,7 +127,7 @@
         packed = jnp.where(lane8 == n, nbr[0, n % 2, n // 2], packed)
     idx_s[...] = packed
     idx_copies = [
-        remote(idx_s, idx_all.at[g], i_send.at[off - 1], i_recv.at[off - 1], x_dev(mod(g + off, 4)))
+        remote(idx_s, idx_all.at[g], i_send.at[0], i_recv.at[0], x_dev(mod(g + off, 4)))
         for off in range(1, 4)
     ]
     for c in idx_copies:
@@ -135,32 +135,39 @@
     idx_local = pltpu.make_async_copy(idx_s, idx_all.at[g], misc.at[0])
     idx_local.start()
 
-    z_order = (4, 3, 5, 2, 6, 1, 7)
+    z_order = (3, 5, 4, 2, 6, 1, 7)
+
+    def both(ref, send, recv):
+        return remote(ref, ref, send, recv, partner)
 
     def z_copy(off, part):
         zz = mod(z + off, 8)
         cols = pl.ds(pl.multiple_of(zz * HS, HS), HS)
         src = (dk, dq, dv)[part].at[0, :, cols]
-        dst = (kf.at[s], qs.at[z], vf.at[s])[part]
-        n = (off - 1) * 3 + part
-        return remote(src, dst, z_send.at[n], z_recv.at[n], z_dev(zz))
-
-    def z_arrival(off, part):
+        dst = (kf.at[core, z], qs.at[z], vf.at[core, z])[part]
+        n = part if part < 2 else 1 + off
+        return remote(src, dst, z_send.at[part], z_recv.at[n], z_dev(zz))
+
+    def z_all(part):
+        ref = (kf.at[core, pl.ds(0, 7)], qs.at[pl.ds(0, 7)], vf.at[core, pl.ds(0, 7)])[part]
+        return both(ref, z_send.at[part], z_recv.at[part])
+
+    def v_arrival(off):
         zz = mod(z + 8 - off, 8)
-        b = 2 * zz + core
-        dst = (kf.at[b], qs.at[zz], vf.at[b])[part]
-        n = (off - 1) * 3 + part
-        return remote(dst, dst, z_send.at[n], z_recv.at[n], z_dev(zz))
-
-    def forward(off, part):
-        ref = (kf, vf)[part].at[2 * mod(z + 8 - off, 8) + core]
-        n = off * 2 + part
-        return remote(ref, ref, f_send.at[n], f_recv.at[n], partner)
-
-    def forward_arrival(off, part):
-        ref = (kf, vf)[part].at[2 * mod(z + 8 - off, 8) + 1 - core]
-        n = off * 2 + part
-        return remote(ref, ref, f_send.at[n], f_recv.at[n], partner)
+        ref = vf.at[core, zz]
+        return remote(ref, ref, z_send.at[2], z_recv.at[1 + off], z_dev(zz))
+
+    def v_forward(off):
+        ref = vf.at[core, mod(z + 8 - off, 8)]
+        return remote(ref, ref, f_send.at[1], f_recv.at[1], partner)
+
+    def forward(part):
+        ref = (kf, vf)[part].at[core]
+        return remote(ref, ref, f_send.at[part], f_recv.at[part], partner)
+
+    def forward_arrival(part):
+        ref = (kf, vf)[part].at[1 - core]
+        return remote(ref, ref, f_send.at[part], f_recv.at[part], partner)
 
     for part in range(3):
         for off in z_order:
@@ -172,15 +179,11 @@
     def y_copy(hc, off):
         return remote(
             kvs[hc].at[off], pool[hc].at[pl.ds(2 * m, 2)],
-            y_send.at[hc * 3 + off], y_recv.at[hc * 3 + off], y_dev(mod(m + 1 + off, 4)),
-        )
-
-    def y_arrival(hc, off):
-        mm = mod(m + 3 - off, 4)
-        return remote(
-            kvs[hc].at[off], pool[hc].at[pl.ds(2 * mm, 2)],
-            y_send.at[hc * 3 + off], y_recv.at[hc * 3 + off], y_dev(mm),
-        )
+            y_send.at[hc], y_recv.at[hc], y_dev(mod(m + 1 + off, 4)),
+        )
+
+    def y_arrivals(hc):
+        return both(pool[hc].at[pl.ds(0, 6)], y_send.at[hc], y_recv.at[hc])
 
     def y_local(hc):
         return pltpu.make_async_copy(kvs[hc].at[3], pool[hc].at[pl.ds(2 * m, 2)], y_loc.at[hc])
@@ -218,15 +221,11 @@
     def q_copy(hc, off):
         mine = qb[hc].at[pl.ds(4 * g, 4)]
         return remote(
-            mine, mine, q_send.at[hc * 3 + off], q_recv.at[hc * 3 + off], x_dev(mod(g + 1 + off, 4))
-        )
-
-    def q_arrival(hc, off):
-        gg = mod(g + 3 - off, 4)
-        theirs = qb[hc].at[pl.ds(4 * gg, 4)]
-        return remote(
-            theirs, theirs, q_send.at[hc * 3 + off], q_recv.at[hc * 3 + off], x_dev(gg)
-        )
+            mine, mine, q_send.at[hc], q_recv.at[hc], x_dev(mod(g + 1 + off, 4))
+        )
+
+    def q_arrivals(hc):
+        return both(qb[hc].at[pl.ds(0, 12)], q_send.at[hc], q_recv.at[hc])
 
     def shift_queries():
         loads[0].wait()
@@ -241,11 +240,7 @@
                 q_copy(hc, off).start()
 
     def tables():
-        for off in range(1, 4):
-            gg = mod(g + 4 - off, 4)
-            remote(
-                idx_s, idx_all.at[gg], i_send.at[off - 1], i_recv.at[off - 1], x_dev(gg)
-            ).wait_recv()
+        both(idx_all.at[pl.ds(0, 3)], i_send.at[0], i_recv.at[0]).wait_recv()
         idx_local.wait()
         to_smem = pltpu.make_async_copy(idx_all, idx_sm, misc.at[1])
         to_smem.start()
@@ -281,13 +276,13 @@
     def o_copy(hc, off):
         return remote(
             os[hc].at[off], o_in[hc].at[pl.ds(4 * g, 4)],
-            o_send.at[hc * 3 + off], o_recv.at[hc * 3 + off], x_dev(mod(g + 1 + off, 4)),
+            o_send.at[hc], o_recv.at[hc], x_dev(mod(g + 1 + off, 4)),
         )
 
     def t_copy(hc, off):
         return remote(
             ss[hc].at[off], st_in[hc].at[g],
-            t_send.at[hc * 3 + off], t_recv.at[hc * 3 + off], x_dev(mod(g + 1 + off, 4)),
+            t_send.at[hc], t_recv.at[hc], x_dev(mod(g + 1 + off, 4)),
         )
 
     def o_local(hc):
@@ -299,9 +294,8 @@
         )
 
     def cross(hc):
-        for off in range(3):
-            y_arrival(hc, off).wait_recv()
-            q_arrival(hc, off).wait_recv()
+        y_arrivals(hc).wait_recv()
+        q_arrivals(hc).wait_recv()
         y_local(hc).wait()
 
         def step(off, carry):
@@ -340,9 +334,9 @@
 
         lax.fori_loop(0, 4, step, 0)
 
-    def b_copy(i, k):
+    def b_copy(i):
         return remote(
-            os_self.at[i], self_out.at[0, :, own], b_send.at[k], b_recv.at[k], z_dev(i)
+            os_self.at[i], self_out.at[0, :, own], b_send.at[0], b_recv.at[0], z_dev(i)
         )
 
     KEYS = 512
@@ -354,7 +348,7 @@
             q = qs[i]
             top = None
             for j in range(i + 1):
-                sc = scores_of(q, kf[2 * j : 2 * j + 2].reshape(KEYS, HS))
+                sc = scores_of(q, jnp.concatenate([kf[0, j], kf[1, j]], axis=0))
                 if j == i:
                     sc = jnp.where(key_iota <= row_iota + core * ROWS, sc, MASKED)
                 sc_buf[j] = sc
@@ -364,37 +358,39 @@
             total = None
             for j in range(i + 1):
                 w = jnp.exp2(sc_buf[j] * SCALE - top)
-                p_buf[i, :, j * KEYS : (j + 1) * KEYS] = w.astype(BF16)
+                for half in range(2):
+                    p_buf[i, half, :, j * ROWS : (j + 1) * ROWS] = w[
+                        :, half * ROWS : (half + 1) * ROWS
+                    ].astype(BF16)
                 low = fold(w, jnp.add)
                 total = low if total is None else total + low
             tot_buf[i] = total
 
+    def values_part(i, half):
+        return jnp.dot(
+            p_buf[i, half, :, 0 : (i + 1) * ROWS],
+            vf[half, 0 : i + 1].reshape((i + 1) * ROWS, HS),
+            preferred_element_type=F32,
+        )
+
     def self_values():
         for i in reversed(range(8)):
-            acc = jnp.dot(
-                p_buf[i, :, 0 : (i + 1) * KEYS],
-                vf[0 : 2 * i + 2].reshape((i + 1) * KEYS, HS),
-                preferred_element_type=F32,
-            )
+            sc_buf[i, :, 0:HS] = values_part(i, core)
+        forward_arrival(1).wait_recv()
+        for i in reversed(range(8)):
+            acc = sc_buf[i, :, 0:HS] + values_part(i, 1 - core)
             total = jnp.sum(tot_buf[i], axis=1, keepdims=True)
             pos = (2 * i + core) * ROWS + lax.broadcasted_iota(jnp.int32, (ROWS, HS), 0)
             os_self[i] = jnp.where(pos < seq_len, acc * (1.0 / total), 0.0).astype(BF16)
-        for k in (3, 2, 4, 1, 5, 0, 6):
-            b_copy(mod(z + 1 + k, 8), k).start()
+        for off in z_order:
+            b_copy(mod(z + off, 8)).start()
         pltpu.make_async_copy(os_self.at[z], self_out.at[0, :, own], misc.at[10]).start()
 
     first_pos = s * ROWS
 
     def o_arrivals(hc):
-        for off in range(3):
-            gg = mod(g + 3 - off, 4)
-            n = hc * 3 + off
-            remote(
-                os[hc].at[off], o_in[hc].at[pl.ds(4 * gg, 4)], o_send.at[n], o_recv.at[n], x_dev(gg)
-            ).wait_recv()
-            remote(
-                ss[hc].at[off], st_in[hc].at[gg], t_send.at[n], t_recv.at[n], x_dev(gg)
-            ).wait_recv()
+        both(o_in[hc].at[pl.ds(0, 12)], o_send.at[hc], o_recv.at[hc]).wait_recv()
+        both(st_in[hc].at[pl.ds(0, 3)], t_send.at[hc], t_recv.at[hc]).wait_recv()
         for c in o_local(hc):
             c.wait()
 
@@ -453,14 +449,12 @@
         out_copy(hc).start()
 
     def sent(hc):
-        for off in range(3):
-            y_copy(hc, off).wait_send()
-            q_copy(hc, off).wait_send()
+        both(kvs[hc].at[pl.ds(0, 3)], y_send.at[hc], y_recv.at[hc]).wait_send()
+        q_arrivals(hc).wait_send()
 
     def answered(hc):
-        for off in range(3):
-            o_copy(hc, off).wait_send()
-            t_copy(hc, off).wait_send()
+        both(os[hc].at[pl.ds(0, 3)], o_send.at[hc], o_recv.at[hc]).wait_send()
+        both(ss[hc].at[pl.ds(0, 3)], t_send.at[hc], t_recv.at[hc]).wait_send()
         tail_copy(hc).wait_send()
 
     for c in loads[1:]:
@@ -471,66 +465,52 @@
         encode(hc)
     for c in local_in:
         c.wait()
-    for part in range(2):
-        forward(0, part).start()
     tables()
     cross(0)
-    for off in z_order:
-        z_arrival(off, 0).wait_recv()
-        forward(off, 0).start()
+    z_all(0).wait_recv()
+    forward(0).start()
+    v_forward(0).start()
     halo_copy.wait_send()
-    for c in idx_copies:
-        c.wait_send()
+    both(idx_all.at[pl.ds(0, 3)], i_send.at[0], i_recv.at[0]).wait_send()
     cross(1)
     sent(0)
-    for off in z_order:
-        z_arrival(off, 1).wait_recv()
-    for off in range(8):
-        forward_arrival(off, 0).wait_recv()
+    z_all(1).wait_recv()
+    forward_arrival(0).wait_recv()
     self_weights()
     cross(2)
     for off in z_order:
-        z_arrival(off, 2).wait_recv()
-        forward(off, 1).start()
+        v_arrival(off).wait_recv()
+        v_forward(off).start()
     sent(1)
-    for off in z_order:
-        for part in range(3):
-            z_copy(off, part).wait_send()
-    for off in range(8):
-        forward_arrival(off, 1).wait_recv()
+    for part in range(3):
+        z_all(part).wait_send()
+    combine(0)
     self_values()
-    combine(0)
     cross(3)
     combine(1)
     cross(4)
     sent(2)
     sent(3)
     sent(4)
-    for off in range(8):
-        for part in range(2):
-            forward(off, part).wait_send()
+    for part in range(2):
+        forward(part).wait_send()
     combine(2)
+    combine(3)
+    combine(4)
+    answered(0)
+    answered(1)
     finish(0)
     finish(1)
-    combine(3)
-    answered(0)
-    answered(1)
     finish(2)
-    combine(4)
     finish(3)
+    finish(4)
     answered(2)
     answered(3)
-    finish(4)
     answered(4)
 
     pltpu.make_async_copy(os_self.at[z], self_out.at[0, :, own], misc.at[10]).wait()
-    for k in range(7):
-        src = mod(z + 7 - k, 8)
-        cols = pl.ds(pl.multiple_of(src * HS, HS), HS)
-        remote(
-            os_self.at[z], self_out.at[0, :, cols], b_send.at[k], b_recv.at[k], z_dev(src)
-        ).wait_recv()
-        b_copy(mod(z + 1 + k, 8), k).wait_send()
+    both(self_out.at[0, :, pl.ds(0, 7 * HS)], b_send.at[0], b_recv.at[0]).wait_recv()
+    both(os_self.at[pl.ds(0, 7)], b_send.at[0], b_recv.at[0]).wait_send()
     for hc in range(CHUNKS):
         out_copy(hc).wait()
 
@@ -569,19 +549,18 @@
         V((ROWS, WIDTH), BF16),
     ]
     scratch += [
-        V((8, ROWS, HS), BF16), V((16, ROWS, HS), BF16), V((16, ROWS, HS), BF16),
-        V((8, ROWS, HS), BF16), V((8, ROWS, 512), F32), V((8, ROWS, 4096), BF16), V((8, ROWS, HS), F32),
+        V((8, ROWS, HS), BF16), V((2, 8, ROWS, HS), BF16), V((2, 8, ROWS, HS), BF16),
+        V((8, ROWS, HS), BF16), V((8, ROWS, 512), F32), V((8, 2, ROWS, 2048), BF16), V((8, ROWS, HS), F32),
     ]
     scratch += [
         V((8, 128), jnp.int32), V((4, 8, 128), jnp.int32), pltpu.SMEM((4, 8, 128), jnp.int32),
         pltpu.SMEM((16,), jnp.int32), pltpu.SMEM((16,), jnp.int32), pltpu.SMEM((8,), jnp.int32),
     ]
-    per = 3 * CHUNKS
     scratch += [
         dma(n)
         for n in (
-            7, 21, 21, 16, 16, per, per, CHUNKS, per, per, per, per, per, per, CHUNKS, CHUNKS,
-            3, 3, 7, 7, 1, 1, CHUNKS, CHUNKS, CHUNKS, 12,
+            7, 3, 9, 2, 2, CHUNKS, CHUNKS, CHUNKS, CHUNKS, CHUNKS, CHUNKS, CHUNKS, CHUNKS, CHUNKS,
+            CHUNKS, CHUNKS, 1, 1, 1, 1, 1, 1, CHUNKS, CHUNKS, CHUNKS, 12,
         )
     ]
     widths = [n * HS for n in HEADS_OF]

time: 75.4 us -> 73.2 us (0.971)
  the two profiles are of different devices: /device:TPU:1 before, /device:TPU:24 now
where the time goes in v4:
time: 73.2 us; the launch traced here: 73.1 us
  Pallas kernels  71.8 us (98%)
  between operations  1.29 us (2%)
    pallas_call x1, Pallas kernels, local(): pl.pallas_call(kernel, out_shape=(shape, shape), in_specs=[smem, smem] +...  69.8 us
    pallas_call x1, Pallas kernels, local(): pl.pallas_call(place, out_shape=(shape, shape), in_specs=[any_] * 2, out_...  1.98 us

profile of v4, /device:TPU:24, one launch (start us, length us, event | category | flops | bytes accessed | tf_op | source)
XLA Modules:
  0.0 73.1 jit_solution(17542413921067445114)
XLA Ops:
  1.3 69.8 %retro_block.1 = (bf16[1,256,1024]{2,1,0:T(8,128)(2,1)}, bf16[1,256,1024]{2,1,0:T(8,128)(2,1)}) custom-call(s32[1,2,4]{2,1,0:T(2,128)} %bitcast.1, s32[1]{0:T(128)S(6)} %copy.11.lens, bf16[1,256,1024]{2,1,0:T(8,128)(2,1)} %dq.1, bf16[1,256,1024]{2,1,0:T(8,128)(2,1)} %dk.1, bf16[1,256,1024]{2,1,0:T(8,128)(2,1)} %dv.1, bf16[1,256,1024]{2,1,0:T(8,128)(2,1)} %cq.1, ...), custom_call_target="tpu_custom_call" | custom-call | tf_op jit(solution)/shard_map/retro_block/pallas_call | solution.py:580
  71.1 2.0 %place.1 = (bf16[1,256,1024]{2,1,0:T(8,128)(2,1)}, bf16[1,256,1024]{2,1,0:T(8,128)(2,1)}) custom-call(bf16[1,256,1024]{2,1,0:T(8,128)(2,1)} %get-tuple-element.4.a_ref, bf16[1,256,1024]{2,1,0:T(8,128)(2,1)} %get-tuple-element.5.b_ref), custom_call_target="tpu_custom_call" | custom-call | tf_op jit(solution)/shard_map/place/pallas_call | solution.py:591

commit v5 on v4

--- a/solution.py
+++ b/solution.py
@@ -11,8 +11,8 @@
 HS = 128
 SPAN = 64
 CAP = 4
-HEADS_OF = (1, 2, 2, 2, 1)
-FIRST = (0, 1, 3, 5, 7)
+HEADS_OF = (1, 2, 2, 1, 1, 1)
+FIRST = (0, 1, 3, 5, 6, 7)
 CHUNKS = len(HEADS_OF)
 ROWS = 256
 WIDTH = 1024
@@ -169,9 +169,8 @@
         ref = (kf, vf)[part].at[1 - core]
         return remote(ref, ref, f_send.at[part], f_recv.at[part], partner)
 
-    for part in range(3):
-        for off in z_order:
-            z_copy(off, part).start()
+    for off in z_order:
+        z_copy(off, 0).start()
 
     def columns(hc):
         return slice(FIRST[hc] * HS, (FIRST[hc] + HEADS_OF[hc]) * HS)
@@ -298,28 +297,36 @@
         q_arrivals(hc).wait_recv()
         y_local(hc).wait()
 
-        def step(off, carry):
-            c = mod(g + 1 + off, 4)
-            heads = range(HEADS_OF[hc])
-            tiles = [(r, j) for r in range(CAP) for j in heads]
-            q2 = [qb[hc][row_tab[c * 4 + r]] for r in range(CAP)]
-            k2 = [pool[hc][id_tab[c * 4 + r], 0] for r in range(CAP)]
-            v2 = [pool[hc][id_tab[c * 4 + r], 1] for r in range(CAP)]
+        heads = range(HEADS_OF[hc])
+        group = 2 if len(heads) == 1 else 1
+
+        def step(turn, carry):
+            tiles = [(a, r, j) for a in range(group) for r in range(CAP) for j in heads]
+            offs = [turn * group + a for a in range(group)]
+            cands = [mod(g + 1 + off, 4) for off in offs]
+            q2 = [[qb[hc][row_tab[c * 4 + r]] for r in range(CAP)] for c in cands]
+            k2 = [[pool[hc][id_tab[c * 4 + r], 0] for r in range(CAP)] for c in cands]
+            v2 = [[pool[hc][id_tab[c * 4 + r], 1] for r in range(CAP)] for c in cands]
 
             def split(x):
-                return [x[r][:, j * HS : (j + 1) * HS] for r, j in tiles]
+                return [x[a][r][:, j * HS : (j + 1) * HS] for a, r, j in tiles]
 
             tops, totals, mixed = attend_all(split(q2), split(k2), split(v2))
             logs = [top * SCALE + jnp.log2(total) for top, total in zip(tops, totals)]
-            for a, (r, j) in enumerate(tiles):
-                os[hc][off, r, :, j * HS : (j + 1) * HS] = mixed[a].astype(BF16)
-            for r in range(CAP):
-                row = jnp.where(lane64 == 0, logs[r * len(heads)], 0.0)
-                for j in heads[1:]:
-                    row = jnp.where(lane64 == j, logs[r * len(heads) + j], row)
-                stage[r * SPAN : (r + 1) * SPAN, :] = row
-            ss[hc][off] = jnp.transpose(stage[...])[0:8]
-
+            for n, (a, r, j) in enumerate(tiles):
+                os[hc][offs[a], r, :, j * HS : (j + 1) * HS] = mixed[n].astype(BF16)
+            for a, off in enumerate(offs):
+                for r in range(CAP):
+                    base = (a * CAP + r) * len(heads)
+                    row = jnp.where(lane64 == 0, logs[base], 0.0)
+                    for j in heads[1:]:
+                        row = jnp.where(lane64 == j, logs[base + j], row)
+                    stage[r * SPAN : (r + 1) * SPAN, :] = row
+                ss[hc][off] = jnp.transpose(stage[...])[0:8]
+                answer(off)
+            return carry
+
+        def answer(off):
             @pl.when(off < 3)
             def _():
                 o_copy(hc, off).start()
@@ -330,9 +337,7 @@
                 for c_ in o_local(hc):
                     c_.start()
 
-            return carry
-
-        lax.fori_loop(0, 4, step, 0)
+        lax.fori_loop(0, 4 // group, step, 0)
 
     def b_copy(i):
         return remote(
@@ -460,6 +465,9 @@
     for c in loads[1:]:
         c.wait()
     encode(0)
+    for part in (1, 2):
+        for off in z_order:
+            z_copy(off, part).start()
     shift_queries()
     for hc in range(1, CHUNKS):
         encode(hc)
@@ -489,14 +497,17 @@
     cross(3)
     combine(1)
     cross(4)
+    combine(2)
+    cross(5)
     sent(2)
     sent(3)
     sent(4)
+    sent(5)
     for part in range(2):
         forward(part).wait_send()
-    combine(2)
     combine(3)
     combine(4)
+    combine(5)
     answered(0)
     answered(1)
     finish(0)
@@ -504,9 +515,11 @@
     finish(2)
     finish(3)
     finish(4)
+    finish(5)
     answered(2)
     answered(3)
     answered(4)
+    answered(5)
 
     pltpu.make_async_copy(os_self.at[z], self_out.at[0, :, own], misc.at[10]).wait()
     both(self_out.at[0, :, pl.ds(0, 7 * HS)], b_send.at[0], b_recv.at[0]).wait_recv()

time: 73.2 us -> 73.1 us (level)
  the two profiles are of different devices: /device:TPU:24 before, /device:TPU:1 now
where the time goes in v5:
time: 73.1 us; the launch traced here: 71.9 us
  Pallas kernels  70.5 us (96%)
  between operations  1.45 us (2%)
    pallas_call x1, Pallas kernels, local(): pl.pallas_call(kernel, out_shape=(shape, shape), in_specs=[smem, smem] +...  68.5 us
    pallas_call x1, Pallas kernels, local(): pl.pallas_call(place, out_shape=(shape, shape), in_specs=[any_] * 2, out_...  1.98 us

profile of v5, /device:TPU:1, one launch (start us, length us, event | category | flops | bytes accessed | tf_op | source)
XLA Modules:
  0.0 71.9 jit_solution(13882009603069069852)
XLA Ops:
  1.3 68.5 %retro_block.1 = (bf16[1,256,1024]{2,1,0:T(8,128)(2,1)}, bf16[1,256,1024]{2,1,0:T(8,128)(2,1)}) custom-call(s32[1,2,4]{2,1,0:T(2,128)} %bitcast.1, s32[1]{0:T(128)S(6)} %copy.11.lens, bf16[1,256,1024]{2,1,0:T(8,128)(2,1)} %dq.1, bf16[1,256,1024]{2,1,0:T(8,128)(2,1)} %dk.1, bf16[1,256,1024]{2,1,0:T(8,128)(2,1)} %dv.1, bf16[1,256,1024]{2,1,0:T(8,128)(2,1)} %cq.1, ...), custom_call_target="tpu_custom_call" | custom-call | tf_op jit(solution)/shard_map/retro_block/pallas_call | solution.py:593
  69.8 2.0 %place.1 = (bf16[1,256,1024]{2,1,0:T(8,128)(2,1)}, bf16[1,256,1024]{2,1,0:T(8,128)(2,1)}) custom-call(bf16[1,256,1024]{2,1,0:T(8,128)(2,1)} %get-tuple-element.4.a_ref, bf16[1,256,1024]{2,1,0:T(8,128)(2,1)} %get-tuple-element.5.b_ref), custom_call_target="tpu_custom_call" | custom-call | tf_op jit(solution)/shard_map/place/pallas_call | solution.py:604
